TPU v7x, 32 devices: a whole 2x2x4 slice. The times are simulated.
32 devices in a mesh: song: 2 (over x), tm: 8 (over z, y), freq: 2 (over core).
Axes of the slice: x: 2, y: 2, z: 4, core: 2. Of those that a mesh axis runs over, the one named last changes fastest.
Arguments:
- latent: bfloat16 [256, 128, 1024], P(None, 'freq', ('song', 'tm')), parts along dimension 2, as said below
- mel_noisy: float32 [128, 1024], P('freq', ('song', 'tm')), parts along dimension 1, may hold values from -6 to 6
- time_shift: float32 [512], P('song'), parts along dimension 0, may hold values from -3 to 3
- first_gain: float32 [256], replicated, may hold values from 0.5 to 1.5
- first_shift: float32 [256], replicated, may hold values from -3 to 3
- conv_first: bfloat16 [3, 3, 256, 256], replicated, may hold values from -0.125 to 0.125
- second_gain: float32 [256], replicated, may hold values from 0.5 to 1.5
- second_shift: float32 [256], replicated, may hold values from -3 to 3
- conv_second: bfloat16 [3, 3, 256, 256], replicated, may hold values from -0.125 to 0.125
- second_bias: float32 [256], replicated, may hold values from -3 to 3
- out_proj: float32 [256], replicated, may hold values from -0.375 to 0.375
- pre_weight: bfloat16 [1536, 7, 128], P('tm'), may hold values from -0.1875 to 0.1875
- pre_bias: float32 [1536], replicated, may hold values from -3 to 3
- up_weight: bfloat16 [1536, 8, 768], P(None, None, 'freq'), may hold values from -0.109375 to 0.109375
- up_bias: float32 [768], P('freq'), may hold values from -3 to 3
Outputs:
- mel_next: float32 [128, 1024], P('freq', ('song', 'tm')), parts along dimension 1
- vocal: bfloat16 [768, 4096], P('freq', ('song', 'tm')), parts along dimension 1
There are 2 independent parts, one for each index of `song`. A program takes and returns all parts, laid end to end along the dimension named above; an argument that names none is the same for every part. Nothing has to cross between parts.
Inputs may be any that keep to these rules, and one draw needn't show every extreme that they name: `latent`: activations of the block's input, of order one to some tens.
All inputs are finite; a program needn't handle non-finite values.
Results may differ from a plain program's by a relative error of at most 0.0055.
Values may be sent and summed in bfloat16 or wider, within the bound.
A program may use at most 192 MiB of HBM per device.

v0:
```python
import jax
import jax.numpy as jnp
from jax import lax
from jax.sharding import PartitionSpec as P

GROUPS = 32


EPSILON = 1e-05
STEP_SIZE = 0.25


def padded_2(x, sides, width):
    for axis, dim in sides:
        devices, length = (lax.axis_size(axis), x.shape[dim])
        up = [(i, (i + 1) % devices) for i in range(devices - 1)]
        down = [(j, i) for i, j in up]
        last = lax.slice_in_dim(x, length - width, length, axis=dim)
        first = lax.slice_in_dim(x, 0, width, axis=dim)
        before = lax.ppermute(last, axis, up)
        after = lax.ppermute(first, axis, down)
        x = jnp.concatenate([before, x, after], axis=dim)
    return x


def group_moments(center):
    chans, bins, frames = center.shape
    values = center.astype(jnp.float32).reshape(GROUPS, chans // GROUPS, bins, frames)
    first = jnp.sum(values, axis=(1, 2, 3))
    second = jnp.sum(values * values, axis=(1, 2, 3))
    first, second = lax.psum((first, second), ("tm", "freq"))
    count = float(chans // GROUPS * bins * frames * lax.axis_size("tm") * lax.axis_size("freq"))
    mean = first / count
    var = second / count - mean * mean
    return (mean, lax.rsqrt(var + EPSILON))


def apply_norm(values_in, mean, scale_inv, gain, shift):
    chans, bins, frames = values_in.shape
    values = values_in.astype(jnp.float32).reshape(GROUPS, chans // GROUPS, bins, frames)
    scaled = (values - mean[:, None, None, None]) * scale_inv[:, None, None, None]
    scaled = scaled.reshape(chans, bins, frames) * gain[:, None, None] + shift[:, None, None]
    return jax.nn.silu(scaled)


def norm_silu(values_in, gain, shift):
    mean, scale_inv = group_moments(values_in)
    return apply_norm(values_in, mean, scale_inv, gain, shift).astype(jnp.bfloat16)


def conv_valid(padded, weight, bins, frames):
    total = jnp.zeros((weight.shape[3], bins, frames), jnp.float32)
    for i in range(3):
        for j in range(3):
            total = total + jnp.einsum(
                "io,ift->oft",
                weight[i, j],
                padded[:, i : i + bins, j : j + frames],
                preferred_element_type=jnp.float32,
            )
    return total


def conv_three(active, weight):
    bins, frames = (active.shape[1], active.shape[2])
    padded = padded_2(active, (("tm", 2), ("freq", 1)), 1)
    return conv_valid(padded, weight, bins, frames)


def up_tap(up_weight, k, feats):
    return jnp.einsum("io,it->ot", up_weight[:, k, :], feats, preferred_element_type=jnp.float32)


def shards(
    latent,
    mel_noisy,
    time_shift,
    first_gain,
    first_shift,
    conv_first,
    second_gain,
    second_shift,
    conv_second,
    second_bias,
    out_proj,
    pre_weight,
    pre_bias,
    up_weight,
    up_bias,
):
    active = norm_silu(latent, first_gain, first_shift)
    first_out = (conv_three(active, conv_first) + time_shift[:, None, None]).astype(jnp.bfloat16)
    second_in = norm_silu(first_out, second_gain, second_shift)
    second_conv = conv_three(second_in, conv_second)
    hidden = latent.astype(jnp.float32) + second_conv + second_bias[:, None, None]
    velocity = jnp.sum(out_proj[:, None, None] * hidden, axis=0)
    mel_next = mel_noisy + STEP_SIZE * velocity
    mel_in = mel_next.astype(jnp.bfloat16)
    mel_full = lax.all_gather(mel_in, "freq", axis=0, tiled=True)
    frames = mel_full.shape[1]
    taps = pre_weight.shape[1]
    extended = padded_2(mel_full, (("tm", 1),), 4)
    piece = lax.all_gather(pre_weight, "tm", axis=0, tiled=True)
    total = jnp.zeros((piece.shape[0], frames + 2), jnp.float32)
    for k in range(taps):
        total = total + jnp.dot(
            piece[:, k, :], extended[:, k : k + frames + 2], preferred_element_type=jnp.float32
        )
    position = lax.axis_index("tm") * frames - 1 + jnp.arange(frames + 2, dtype=jnp.int32)
    valid = (position >= 0) & (position < frames * lax.axis_size("tm"))
    features = jnp.where(valid[None, :], total + pre_bias[:, None], 0.0).astype(jnp.bfloat16)
    middle = features[:, 1 : frames + 1]
    before = features[:, 0:frames]
    after = features[:, 2 : frames + 2]
    phases = []
    for p in range(4):
        term = up_tap(up_weight, p + 2, middle)
        if p <= 1:
            term = term + up_tap(up_weight, p + 6, before)
        else:
            term = term + up_tap(up_weight, p - 2, after)
        phases.append(term)
    stacked = jnp.stack(phases, axis=2).reshape(up_weight.shape[2], 4 * frames)
    vocal = (stacked + up_bias[:, None]).astype(jnp.bfloat16)
    return (mel_next, vocal)


def solution(mesh):
    in_specs = (
        P(None, "freq", ("song", "tm")),
        P("freq", ("song", "tm")),
        P("song"),
        P(),
        P(),
        P(),
        P(),
        P(),
        P(),
        P(),
        P(),
        P("tm", None, None),
        P(),
        P(None, None, "freq"),
        P("freq"),
    )
    out_specs = (P("freq", ("song", "tm")), P("freq", ("song", "tm")))
    return jax.shard_map(shards, mesh=mesh, in_specs=in_specs, out_specs=out_specs, check_vma=False)
```

profile of v0, /device:TPU:0, one launch (start us, length us, event | category | flops | bytes accessed | tf_op | source)
XLA Modules:
  0.0 244.6 jit_solution(2898610104928867192)
XLA Ops:
  7.2 2.2 convert_reduce_fusion
  9.8 34.9 %all-reduce.1 = (f32[32]{0:T(128)S(1)}, f32[32]{0:T(128)S(1)}) all-reduce(f32[32]{0:T(128)S(1)} %reduce_sum.62, f32[32]{0:T(128)S(1)} %reduce_sum.59), channel_id=1, replica_groups=mesh['song'=2,'tm'=8,'freq'=2] {'tm','freq'}, use_global_device_ids=true, to_apply=%region_5.6 | all-reduce | flops 64 | bytes 512 | tf_op jit(solution)/shard_map/psum | solution.py:31
  45.1 3.0 %fusion.19 = bf16[256,64,64]{0,2,1:T(8,128)(2,1)S(1)} fusion(bf16[256,64,64]{0,2,1:T(8,128)(2,1)} %param.15, f32[256]{0:T(256)} %param.19, f32[256]{0:T(256)} %param.18, f32[256]{0:T(256)S(1)} %mul.84, f32[256]{0:T(256)S(1)} %sub.36), kind=kLoop, calls=%fused_computation.26 | loop fusion | flops 10485760 | bytes 4198400 | tf_op jit(solution)/shard_map/convert_element_type | solution.py:48
  48.2 1.3 collective-permute-start
  49.5 1.3 collective-permute-start.1
  50.9 44.2 %fusion.172 = (bf16[1536,1,384]{2,1,0:T(2,128)(2,1)}, bf16[1536,1,384]{2,1,0:T(2,128)(2,1)}, bf16[1536,1,384]{2,1,0:T(2,128)(2,1)}, bf16[1536,1,384]{2,1,0:T(2,1...) fusion(bf16[1536,8,384]{2,1,0:T(8,128)(2,1)} %param.28), kind=kLoop, calls=%fused_computation.218 | loop fusion | bytes 18874368 | tf_op jit(solution)/shard_map/slice | solution.py:71
  95.1 2.6 %fusion.109 = f32[64,64,256]{2,1,0:T(8,128)} fusion(bf16[256,64,64]{0,2,1:T(8,128)(2,1)S(1)} %fusion.19, bf16[3,3,256,256]{3,2,1,0:T(8,128)(2,1)S(1)} %copy-done.10), kind=kOutput, calls=%fused_computation.139 | convolution fusion | flops 536870912 | bytes 6422528 | tf_op jit(solution)/shard_map/io,ift->oft/dot_general | solution.py:55
  97.7 1.3 collective-permute-start.2
  99.0 1.5 collective-permute-start.3
  100.5 2.7 %fusion.59 = f32[64,64,256]{2,1,0:T(8,128)} fusion(bf16[256,64,1]{0,2,1:T(2,128)(2,1)S(1)} %collective-permute-done.1, bf16[256,64,64]{0,2,1:T(8,128)(2,1)S(1)} %fusion.19, bf16[3,3,256,256]{3,2,1,0:T(8,128)(2,1)S(1)} %copy-done.10), kind=kOutput, calls=%fused_computation.71 | convolution fusion | flops 541065216 | bytes 6488064 | tf_op jit(solution)/shard_map/io,ift->oft/dot_general | solution.py:55
  103.2 2.7 %fusion.61 = f32[64,64,256]{2,1,0:T(8,128)} fusion(bf16[256,64,64]{0,2,1:T(8,128)(2,1)S(1)} %fusion.19, bf16[256,64,1]{0,2,1:T(2,128)(2,1)S(1)} %collective-permute-done, bf16[3,3,256,256]{3,2,1,0:T(8,128)(2,1)S(1)} %copy-done.10), kind=kOutput, calls=%fused_computation.74 | convolution fusion | flops 541065216 | bytes 6488064 | tf_op jit(solution)/shard_map/io,ift->oft/dot_general | solution.py:55
  105.9 2.8 %maximum_maximum_fusion = (bf16[256,65,66]{0,2,1:T(8,128)(2,1)S(1)}, bf16[256,65,66]{0,2,1:T(8,128)(2,1)S(1)}) fusion(bf16[256,64,1]{0,2,1:T(2,128)(2,1)S(1)} %collective-permute-done.1, bf16[256,64,64]{0,2,1:T(8,128)(2,1)S(1)} %fusion.19, bf16[256,64,1]{0,2,1:T(2,128)(2,1)S(1)} %collective-permute-done, bf16[256,1,66]{0,2,1:T(8,128)(2,1)S(1)} %collective-permute-done.2, ...), kind=kLoop, calls=%fused_computation.32 | loop fusion | flops 17571840 | bytes 6623232 | tf_op jit(solution)/shard_map/concatenate | solution.py:22
  108.7 2.7 %fusion.55 = f32[64,64,256]{2,1,0:T(8,128)} fusion(bf16[256,65,66]{0,2,1:T(8,128)(2,1)S(1)} %get-tuple-element.27, bf16[3,3,256,256]{3,2,1,0:T(8,128)(2,1)S(1)} %copy-done.10), kind=kOutput, calls=%fused_computation.66 | convolution fusion | flops 536870912 | bytes 6422528 | tf_op jit(solution)/shard_map/io,ift->oft/dot_general | solution.py:55
  111.4 2.7 %fusion.57 = f32[64,64,256]{2,1,0:T(8,128)} fusion(bf16[256,65,66]{0,2,1:T(8,128)(2,1)S(1)} %get-tuple-element.27, bf16[3,3,256,256]{3,2,1,0:T(8,128)(2,1)S(1)} %copy-done.10), kind=kOutput, calls=%fused_computation.68 | convolution fusion | flops 536870912 | bytes 6422528 | tf_op jit(solution)/shard_map/io,ift->oft/dot_general | solution.py:55
  114.0 2.7 %fusion.63 = f32[64,64,256]{2,1,0:T(8,128)} fusion(bf16[256,65,66]{0,2,1:T(8,128)(2,1)S(1)} %get-tuple-element.26, bf16[3,3,256,256]{3,2,1,0:T(8,128)(2,1)S(1)} %copy-done.10), kind=kOutput, calls=%fused_computation.76 | convolution fusion | flops 536870912 | bytes 6422528 | tf_op jit(solution)/shard_map/io,ift->oft/dot_general | solution.py:55
  116.7 2.7 %fusion.65 = f32[64,64,256]{2,1,0:T(8,128)} fusion(bf16[256,65,66]{0,2,1:T(8,128)(2,1)S(1)} %get-tuple-element.26, bf16[3,3,256,256]{3,2,1,0:T(8,128)(2,1)S(1)} %copy-done.10), kind=kOutput, calls=%fused_computation.78 | convolution fusion | flops 536870912 | bytes 6422528 | tf_op jit(solution)/shard_map/io,ift->oft/dot_general | solution.py:55
  119.4 2.8 %fusion.67 = f32[64,64,256]{2,1,0:T(8,128)} fusion(bf16[256,65,66]{0,2,1:T(8,128)(2,1)S(1)} %get-tuple-element.26, bf16[3,3,256,256]{3,2,1,0:T(8,128)(2,1)S(1)} %copy-done.10), kind=kOutput, calls=%fused_computation.80 | convolution fusion | flops 536870912 | bytes 6422528 | tf_op jit(solution)/shard_map/io,ift->oft/dot_general | solution.py:55
  122.9 10.8 %convert_reduce_fusion.1 = (f32[256]{0:T(256)S(1)}, f32[256]{0:T(256)S(1)}, bf16[64,64,256]{2,1,0:T(8,128)(2,1)S(1)}) fusion(f32[256]{0:T(256)S(1)} %copy-done.14, bf16[3,3,256,256]{3,2,1,0:T(8,128)(2,1)} %param.20, bf16[256,65,66]{0,2,1:T(8,128)(2,1)S(1)} %get-tuple-element.27, f32[64,64,256]{2,1,0:T(8,128)} %fusion.55, f32[64,64,256]{2,1,0:T(8,128)} %fusion.57, ...), kind=kOutput, calls=%fused_computation.5 | convolution fusion | flops 551550464 | bytes 37882880 | tf_op jit(solution)/shard_map/io,ift->oft/dot_general | solution.py:55
  134.2 33.4 %all-reduce = (f32[32]{0:T(128)S(1)}, f32[32]{0:T(128)S(1)}) all-reduce(f32[32]{0:T(128)S(1)} %reduce_sum.84, f32[32]{0:T(128)S(1)} %reduce_sum.81), channel_id=1, replica_groups=mesh['song'=2,'tm'=8,'freq'=2] {'tm','freq'}, use_global_device_ids=true, to_apply=%region_11.12 | all-reduce | flops 64 | bytes 512 | tf_op jit(solution)/shard_map/psum | solution.py:31
  167.9 1.4 fusion.10
  169.5 1.3 collective-permute-start.4
  170.8 1.4 collective-permute-start.5
  172.2 1.6 fusion.99
  173.9 3.2 %collective-permute-done.5 = bf16[256,64,1]{0,2,1:T(2,128)(2,1)S(1)} collective-permute-done((bf16[256,64,1]{0,2,1:T(2,128)(2,1)S(1)}, bf16[256,64,1]{0,2,1:T(2,128)(2,1)S(1)}, u32[]{:S(2)}, u32[]{:S(2)}) %collective-permute-start.5) | collective-permute-done | bytes 32800 | tf_op jit(solution)/shard_map/ppermute | solution.py:21
  177.1 1.3 collective-permute-start.6
  178.4 1.5 collective-permute-start.7
  180.0 2.7 %fusion.43 = f32[64,64,256]{2,1,0:T(8,128)} fusion(bf16[256,64,64]{0,2,1:T(8,128)(2,1)S(1)} %fusion.10, bf16[256,64,1]{0,2,1:T(2,128)(2,1)S(1)} %collective-permute-done.4, bf16[3,3,256,256]{3,2,1,0:T(8,128)(2,1)S(1)} %copy-done.11), kind=kOutput, calls=%fused_computation.56 | convolution fusion | flops 541065216 | bytes 6488064 | tf_op jit(solution)/shard_map/io,ift->oft/dot_general | solution.py:55
  182.6 2.7 %fusion.41 = f32[64,64,256]{2,1,0:T(8,128)} fusion(bf16[256,64,1]{0,2,1:T(2,128)(2,1)S(1)} %collective-permute-done.5, bf16[256,64,64]{0,2,1:T(8,128)(2,1)S(1)} %fusion.10, bf16[3,3,256,256]{3,2,1,0:T(8,128)(2,1)S(1)} %copy-done.11), kind=kOutput, calls=%fused_computation.53 | convolution fusion | flops 541065216 | bytes 6488064 | tf_op jit(solution)/shard_map/io,ift->oft/dot_general | solution.py:55
  185.3 2.8 %maximum_maximum_fusion.1 = (bf16[256,65,66]{0,2,1:T(8,128)(2,1)S(1)}, bf16[256,65,66]{0,2,1:T(8,128)(2,1)S(1)}) fusion(bf16[256,64,1]{0,2,1:T(2,128)(2,1)S(1)} %collective-permute-done.5, bf16[256,64,64]{0,2,1:T(8,128)(2,1)S(1)} %fusion.10, bf16[256,64,1]{0,2,1:T(2,128)(2,1)S(1)} %collective-permute-done.4, ...), kind=kLoop, calls=%fused_computation.34 | loop fusion | flops 17571840 | bytes 6623232 | tf_op jit(solution)/shard_map/concatenate | solution.py:22
  188.2 2.7 %fusion.37 = f32[64,64,256]{2,1,0:T(8,128)} fusion(bf16[256,65,66]{0,2,1:T(8,128)(2,1)S(1)} %get-tuple-element.23, bf16[3,3,256,256]{3,2,1,0:T(8,128)(2,1)S(1)} %copy-done.11), kind=kOutput, calls=%fused_computation.48 | convolution fusion | flops 536870912 | bytes 6422528 | tf_op jit(solution)/shard_map/io,ift->oft/dot_general | solution.py:55
  190.8 2.7 %fusion.39 = f32[64,64,256]{2,1,0:T(8,128)} fusion(bf16[256,65,66]{0,2,1:T(8,128)(2,1)S(1)} %get-tuple-element.23, bf16[3,3,256,256]{3,2,1,0:T(8,128)(2,1)S(1)} %copy-done.11), kind=kOutput, calls=%fused_computation.50 | convolution fusion | flops 536870912 | bytes 6422528 | tf_op jit(solution)/shard_map/io,ift->oft/dot_general | solution.py:55
  193.5 2.7 %fusion.45 = f32[64,64,256]{2,1,0:T(8,128)} fusion(bf16[256,65,66]{0,2,1:T(8,128)(2,1)S(1)} %get-tuple-element.22, bf16[3,3,256,256]{3,2,1,0:T(8,128)(2,1)S(1)} %copy-done.11), kind=kOutput, calls=%fused_computation.58 | convolution fusion | flops 536870912 | bytes 6422528 | tf_op jit(solution)/shard_map/io,ift->oft/dot_general | solution.py:55
  196.2 2.7 %fusion.47 = f32[64,64,256]{2,1,0:T(8,128)} fusion(bf16[256,65,66]{0,2,1:T(8,128)(2,1)S(1)} %get-tuple-element.22, bf16[3,3,256,256]{3,2,1,0:T(8,128)(2,1)S(1)} %copy-done.11), kind=kOutput, calls=%fused_computation.60 | convolution fusion | flops 536870912 | bytes 6422528 | tf_op jit(solution)/shard_map/io,ift->oft/dot_general | solution.py:55
  198.9 2.7 %fusion.49 = f32[64,64,256]{2,1,0:T(8,128)} fusion(bf16[256,65,66]{0,2,1:T(8,128)(2,1)S(1)} %get-tuple-element.22, bf16[3,3,256,256]{3,2,1,0:T(8,128)(2,1)S(1)} %copy-done.11), kind=kOutput, calls=%fused_computation.62 | convolution fusion | flops 536870912 | bytes 6422528 | tf_op jit(solution)/shard_map/io,ift->oft/dot_general | solution.py:55
  201.5 10.9 %fusion.23 = f32[64,64]{1,0:T(8,128)S(1)} fusion(bf16[256,64,64]{0,2,1:T(8,128)(2,1)S(1)} %copy-done, f32[64,64,256]{2,1,0:T(8,128)} %fusion.37, f32[64,64,256]{2,1,0:T(8,128)} %fusion.39, f32[64,64,256]{2,1,0:T(8,128)} %fusion.41, f32[64,64,256]{2,1,0:T(8,128)S(1)} %fusion.99, f32[64,64,256]{2,1,0:T(8,128)} %fusion.43, f32[64,64,256]{2,1,0:T(8,128)} %fusion.45, ...), kind=kOutput, calls=%fused_computation.30 | convolution fusion | flops 550498304 | bytes 37898240 | tf_op jit(solution)/shard_map/io,ift->oft/dot_general | solution.py:55
  212.4 1.4 fusion.171
  213.8 2.6 %all_gather.6 = bf16[128,64]{1,0:T(8,128)(2,1)S(1)} all-gather(bf16[64,64]{1,0:T(8,128)(2,1)S(1)} %get-tuple-element.12), channel_id=1, replica_groups=mesh['song'=2,'tm'=8,'freq'=2] {'freq'}, dimensions={0}, use_global_device_ids=true | all-gather | bytes 24576 | tf_op jit(solution)/shard_map/all_gather | solution.py:99
  216.4 1.6 collective-permute-start.8
  218.0 1.3 collective-permute-start.9
  219.6 1.4 fusion.90
  221.0 1.4 fusion.89
  222.4 1.4 collective-permute-done.9
  223.8 1.6 fusion.88
  225.4 1.4 fusion.87
  226.8 1.6 fusion.86
  228.4 1.4 fusion.85
  229.8 1.6 fusion.32
  236.9 0.8 copy.26
  (81 shorter events, 8.3 us)
Async XLA Ops:
  7.2 212.4 %all-gather.2.cloned.1.call-start = ((), (), s32[]{:S(2)}) async-start(), calls=%async_computation | async-start | bytes 3096576 | tf_op jit(solution)/shard_map/all_gather | solution.py:103
  48.2 49.5 %collective-permute-start = (bf16[256,64,1]{0,2,1:T(2,128)(2,1)S(1)}, bf16[256,64,1]{0,2,1:T(2,128)(2,1)S(1)}, u32[]{:S(2)}, u32[]{:S(2)}) collective-permute-start(bf16[256,64,1]{0,2,1:T(2,128)(2,1)S(1)} %get-tuple-element.32), channel_id=1, source_target_pairs={{0,2},{2,4},{4,6},{6,8},{8,10},{10,12},{12,14},{1,3},{3,5},{5,7},{... | collective-permute-start | bytes 98312 | tf_op jit(solution)/shard_map/ppermute | solution.py:20
  49.5 48.2 %collective-permute-start.1 = (bf16[256,64,1]{0,2,1:T(2,128)(2,1)S(1)}, bf16[256,64,1]{0,2,1:T(2,128)(2,1)S(1)}, u32[]{:S(2)}, u32[]{:S(2)}) collective-permute-start(bf16[256,64,1]{0,2,1:T(2,128)(2,1)S(1)} %get-tuple-element.33), channel_id=1, source_target_pairs={{2,0},{4,2},{6,4},{8,6},{10,8},{12,10},{14,12},{3,1},{5,3},{7,5},{... | collective-permute-start | bytes 98312 | tf_op jit(solution)/shard_map/ppermute | solution.py:21
  50.9 44.2 %copy-start.10 = (bf16[3,3,256,256]{3,2,1,0:T(8,128)(2,1)S(1)}, bf16[3,3,256,256]{3,2,1,0:T(8,128)(2,1)}, u32[]{:S(2)}) copy-start(bf16[3,3,256,256]{3,2,1,0:T(8,128)(2,1)} %param.20) | copy-start | bytes 3538948
  97.7 8.1 %collective-permute-start.2 = (bf16[256,1,66]{0,2,1:T(8,128)(2,1)S(1)}, bf16[256,1,66]{0,2,1:T(8,128)(2,1)S(1)}, u32[]{:S(2)}, u32[]{:S(2)}) collective-permute-start(bf16[256,1,66]{0,2,1:T(8,128)(2,1)S(1)} %get-tuple-element.28), channel_id=1, source_target_pairs={{0,1},{2,3},{4,5},{6,7},{8,9},{10,11},{12,13},{14,15},{16,17},{18,... | collective-permute-start | bytes 101384 | tf_op jit(solution)/shard_map/ppermute | solution.py:20
  99.0 6.8 %collective-permute-start.3 = (bf16[256,1,66]{0,2,1:T(8,128)(2,1)S(1)}, bf16[256,1,66]{0,2,1:T(8,128)(2,1)S(1)}, u32[]{:S(2)}, u32[]{:S(2)}) collective-permute-start(bf16[256,1,66]{0,2,1:T(8,128)(2,1)S(1)} %get-tuple-element.29), channel_id=1, source_target_pairs={{1,0},{3,2},{5,4},{7,6},{9,8},{11,10},{13,12},{15,14},{17,16},{19,... | collective-permute-start | bytes 101384 | tf_op jit(solution)/shard_map/ppermute | solution.py:21
  119.4 3.5 %copy-start.1 = (f32[64,64,256]{2,1,0:T(8,128)S(1)}, f32[64,64,256]{2,1,0:T(8,128)}, u32[]{:S(2)}) copy-start(f32[64,64,256]{2,1,0:T(8,128)} %fusion.109) | copy-start | bytes 12582916
  119.4 3.5 %copy-start.14 = (f32[256]{0:T(256)S(1)}, f32[256]{0:T(256)}, u32[]{:S(2)}) copy-start(f32[256]{0:T(256)} %param.17) | copy-start | bytes 3076
  122.9 45.0 %copy-start.15 = (f32[256]{0:T(256)S(1)}, f32[256]{0:T(256)}, u32[]{:S(2)}) copy-start(f32[256]{0:T(256)} %param.22) | copy-start | bytes 3076
  122.9 45.0 %copy-start.16 = (f32[256]{0:T(256)S(1)}, f32[256]{0:T(256)}, u32[]{:S(2)}) copy-start(f32[256]{0:T(256)} %param.21) | copy-start | bytes 3076
  169.5 4.4 %collective-permute-start.4 = (bf16[256,64,1]{0,2,1:T(2,128)(2,1)S(1)}, bf16[256,64,1]{0,2,1:T(2,128)(2,1)S(1)}, u32[]{:S(2)}, u32[]{:S(2)}) collective-permute-start(bf16[256,64,1]{0,2,1:T(2,128)(2,1)S(1)} %get-tuple-element.30), channel_id=1, source_target_pairs={{0,2},{2,4},{4,6},{6,8},{8,10},{10,12},{12,14},{1,3},{3,5},{5,7},{... | collective-permute-start | bytes 98312 | tf_op jit(solution)/shard_map/ppermute | solution.py:20
  170.8 9.2 %copy-start.11 = (bf16[3,3,256,256]{3,2,1,0:T(8,128)(2,1)S(1)}, bf16[3,3,256,256]{3,2,1,0:T(8,128)(2,1)}, u32[]{:S(2)}) copy-start(bf16[3,3,256,256]{3,2,1,0:T(8,128)(2,1)} %param.23) | copy-start | bytes 3538948
  170.8 6.3 %collective-permute-start.5 = (bf16[256,64,1]{0,2,1:T(2,128)(2,1)S(1)}, bf16[256,64,1]{0,2,1:T(2,128)(2,1)S(1)}, u32[]{:S(2)}, u32[]{:S(2)}) collective-permute-start(bf16[256,64,1]{0,2,1:T(2,128)(2,1)S(1)} %get-tuple-element.31), channel_id=1, source_target_pairs={{2,0},{4,2},{6,4},{8,6},{10,8},{12,10},{14,12},{3,1},{5,3},{7,5},{... | collective-permute-start | bytes 98312 | tf_op jit(solution)/shard_map/ppermute | solution.py:21
  177.1 8.2 %collective-permute-start.6 = (bf16[256,1,66]{0,2,1:T(8,128)(2,1)S(1)}, bf16[256,1,66]{0,2,1:T(8,128)(2,1)S(1)}, u32[]{:S(2)}, u32[]{:S(2)}) collective-permute-start(bf16[256,1,66]{0,2,1:T(8,128)(2,1)S(1)} %get-tuple-element.24), channel_id=1, source_target_pairs={{0,1},{2,3},{4,5},{6,7},{8,9},{10,11},{12,13},{14,15},{16,17},{18,... | collective-permute-start | bytes 101384 | tf_op jit(solution)/shard_map/ppermute | solution.py:20
  178.4 6.9 %collective-permute-start.7 = (bf16[256,1,66]{0,2,1:T(8,128)(2,1)S(1)}, bf16[256,1,66]{0,2,1:T(8,128)(2,1)S(1)}, u32[]{:S(2)}, u32[]{:S(2)}) collective-permute-start(bf16[256,1,66]{0,2,1:T(8,128)(2,1)S(1)} %get-tuple-element.25), channel_id=1, source_target_pairs={{1,0},{3,2},{5,4},{7,6},{9,8},{11,10},{13,12},{15,14},{17,16},{19,... | collective-permute-start | bytes 101384 | tf_op jit(solution)/shard_map/ppermute | solution.py:21
  198.9 2.7 %copy-start = (bf16[256,64,64]{0,2,1:T(8,128)(2,1)S(1)}, bf16[256,64,64]{0,2,1:T(8,128)(2,1)}, u32[]{:S(2)}) copy-start(bf16[256,64,64]{0,2,1:T(8,128)(2,1)} %param.15) | copy-start | bytes 6291460
  216.4 3.1 %collective-permute-start.8 = (bf16[128,4]{1,0:T(8,128)(2,1)S(1)}, bf16[128,4]{1,0:T(8,128)(2,1)S(1)}, u32[]{:S(2)}, u32[]{:S(2)}) collective-permute-start(bf16[128,4]{1,0:T(8,128)(2,1)S(1)} %get-tuple-element.34), channel_id=1, source_target_pairs={{0,2},{2,4},{4,6},{6,8},{8,10},{10,12},{12,14},{1,3},{3,5},{5,7},{... | collective-permute-start | bytes 3080 | tf_op jit(solution)/shard_map/ppermute | solution.py:20
  218.0 5.8 %collective-permute-start.9 = (bf16[128,4]{1,0:T(8,128)(2,1)S(1)}, bf16[128,4]{1,0:T(8,128)(2,1)S(1)}, u32[]{:S(2)}, u32[]{:S(2)}) collective-permute-start(bf16[128,4]{1,0:T(8,128)(2,1)S(1)} %get-tuple-element.35), channel_id=1, source_target_pairs={{2,0},{4,2},{6,4},{8,6},{10,8},{12,10},{14,12},{3,1},{5,3},{7,5},{... | collective-permute-start | bytes 3080 | tf_op jit(solution)/shard_map/ppermute | solution.py:21
  221.0 8.8 %copy-start.12 = (f32[1536]{0:T(1024)S(1)}, f32[1536]{0:T(1024)}, u32[]{:S(2)}) copy-start(f32[1536]{0:T(1024)} %param.27) | copy-start | bytes 18436
  223.8 7.6 %copy-start.9 = (bf16[1536,1,384]{2,1,0:T(2,128)(2,1)S(1)}, bf16[1536,1,384]{2,1,0:T(2,128)(2,1)}, u32[]{:S(2)}) copy-start(bf16[1536,1,384]{2,1,0:T(2,128)(2,1)} %get-tuple-element.20) | copy-start | bytes 3538948
  226.8 5.0 %copy-start.8 = (bf16[1536,1,384]{2,1,0:T(2,128)(2,1)S(1)}, bf16[1536,1,384]{2,1,0:T(2,128)(2,1)}, u32[]{:S(2)}) copy-start(bf16[1536,1,384]{2,1,0:T(2,128)(2,1)} %get-tuple-element.18) | copy-start | bytes 3538948
  229.8 2.3 copy-start.7
  231.5 1.7 copy-start.6
  231.8 2.1 copy-start.5
  232.2 2.6 %copy-start.4 = (bf16[1536,1,384]{2,1,0:T(2,128)(2,1)S(1)}, bf16[1536,1,384]{2,1,0:T(2,128)(2,1)}, u32[]{:S(2)}) copy-start(bf16[1536,1,384]{2,1,0:T(2,128)(2,1)} %get-tuple-element.19) | copy-start | bytes 3538948
  233.2 2.3 copy-start.3
  233.9 2.2 copy-start.2
  235.8 1.1 copy-start.13
Sparse Core Ops, SparseCore 0:
  51.0 55.3 all-gather.1
where the time goes:
time: 245 us
  matrix products  76.5 us (31%)
  blocking collectives  70.9 us (29%)
  local copies, waits for them, and re-layouts  49.7 us (20%)
  between operations  14.5 us (6%)
  other arithmetic  14.3 us (6%)
  starting transfers between devices  13.8 us (6%)
  waiting for transfers between devices  4.92 us (2%)
    psum x2, blocking collectives, group_moments(): first, second = lax.psum((first, second), ('tm', 'freq'))  68.3 us
    dot_general x18, matrix products, conv_valid(): jnp.einsum('io,ift->oft', weight[i, j], padded[:, i:i + bins, j:j + frame...  63.5 us
    slice x1, local copies, waits for them, and re-layouts, up_tap(): up_weight[:, k, :]  44.2 us
    dot_general x7, matrix products, shards(): jnp.dot(piece[:, k, :], extended[:, k:k + frames + 2], preferred_element_...  10.4 us
    ppermute x5, starting transfers between devices, padded_2(): after = lax.ppermute(first, axis, down)  6.99 us
    ppermute x5, starting transfers between devices, padded_2(): before = lax.ppermute(last, axis, up)  6.73 us
    concatenate x2, other arithmetic, padded_2(): x = jnp.concatenate([before, x, after], axis=dim)  5.65 us
  transfers between devices with their start and end apart: 11, of which 3 were waited for; matrix products, arithmetic and copies ran while one was open for 49% of the time, Pallas kernels for 0%

commit v1 on v0

v1 whole, which is shorter than its diff:
```python
import functools

import jax
import jax.numpy as jnp
from jax import lax
from jax.experimental import pallas as pl
from jax.experimental.pallas import tpu as pltpu
from jax.sharding import PartitionSpec as P

GROUPS = 32
EPSILON = 1e-05
STEP_SIZE = 0.25
MESH = pl.DeviceIdType.MESH
F32 = jnp.float32
BF16 = jnp.bfloat16
NT = (((1,), (1,)), ((), ()))


def dot(a, b):
    return jnp.dot(a, b, preferred_element_type=F32)


def dot_nt(a, b):
    return lax.dot_general(a, b, NT, preferred_element_type=F32)


def three_parts(x):
    hi = x.astype(BF16)
    rest = x - hi.astype(F32)
    mid = rest.astype(BF16)
    low = (rest - mid.astype(F32)).astype(BF16)
    return hi, mid, low


def block_kernel(
    n_tm, n_f,
    lat, mel, tshift, gain1, shift1, w1, gain2, shift2, w2, bias2, proj,
    mel_out, mt_out,
    stats1, stats2, stage_l, stage_r, halo_l, halo_r, halo_b, corner_l, corner_r,
    act_l, act_r, spread, first, gpad, zt, z_part, z_before, z_after, turned,
    s1_send, s1_recv, s2_send, s2_recv, h_send, h_recv, z_send, z_recv,
):
    bins, frames, chans = lat.shape
    n = n_tm * n_f
    tm = lax.axis_index("tm")
    f = lax.axis_index("freq")
    me = tm * n_f + f
    other = 1 - f
    has_left = tm > 0
    has_right = tm < n_tm - 1

    def peer_of(k):
        p = lax.rem(me + k, n)
        return p, {"tm": p // n_f, "freq": lax.rem(p, n_f)}

    barrier = pltpu.get_barrier_semaphore()

    def greet(k, c):
        pl.semaphore_signal(barrier, inc=1, device_id=peer_of(k)[1], device_id_type=MESH)
        return c

    lax.fori_loop(1, n, greet, 0)

    sub8 = lax.broadcasted_iota(jnp.int32, (bins, 8, chans), 1)
    head = lat[:, 0:16, :].astype(F32)[:, 0:8, :]
    tail = lat[:, frames - 16 : frames, :].astype(F32)[:, 8:16, :]
    stage_l[...] = jnp.sum(jnp.where(sub8 == 0, head, 0.0), axis=1).astype(BF16)
    stage_r[...] = jnp.sum(jnp.where(sub8 == 7, tail, 0.0), axis=1).astype(BF16)

    pl.semaphore_wait(barrier, n - 1)

    def remote(src, dst, send, recv, to):
        return pltpu.make_async_remote_copy(
            src_ref=src, dst_ref=dst, send_sem=send, recv_sem=recv, device_id=to, device_id_type=MESH
        )

    edge = pl.multiple_of((1 - f) * (bins - 16), 16)
    to_left = [{"tm": tm - 1, "freq": f}, {"tm": tm - 1, "freq": other}]
    to_right = [{"tm": tm + 1, "freq": f}, {"tm": tm + 1, "freq": other}]
    partner = {"tm": tm, "freq": other}
    h_bin = remote(lat.at[(1 - f) * (bins - 1)], halo_b, h_send.at[0], h_recv.at[0], partner)
    h_bin.start()
    go_left = [
        remote(stage_l, halo_r, h_send.at[1], h_recv.at[1], to_left[0]),
        remote(stage_l.at[pl.ds(edge, 16)], corner_r, h_send.at[2], h_recv.at[2], to_left[1]),
    ]
    go_right = [
        remote(stage_r, halo_l, h_send.at[3], h_recv.at[3], to_right[0]),
        remote(stage_r.at[pl.ds(edge, 16)], corner_l, h_send.at[4], h_recv.at[4], to_right[1]),
    ]

    @pl.when(has_left)
    def _():
        for c in go_left:
            c.start()

    @pl.when(has_right)
    def _():
        for c in go_right:
            c.start()

    def fold(x):
        return jnp.sum(x.reshape(-1, 8, chans), axis=0)

    def stat_step(b, carry):
        s, q = carry
        x = lat[pl.ds(b * 4, 4)].astype(F32)
        return s + fold(x), q + fold(x * x)

    zero8 = jnp.zeros((8, chans), F32)
    s, q = lax.fori_loop(0, bins // 4, stat_step, (zero8, zero8))

    def send_stats(s, q, stats, send, recv):
        stats[me] = jnp.concatenate(
            [jnp.sum(s, axis=0, keepdims=True), jnp.sum(q, axis=0, keepdims=True)], axis=1
        )

        def go(k, c):
            _, to = peer_of(k)
            remote(stats.at[me], stats.at[me], send.at[k], recv.at[me], to).start()
            return c

        lax.fori_loop(1, n, go, 0)

    def take_stats(stats, send, recv):
        def wait(k, c):
            p, to = peer_of(k)
            remote(stats.at[me], stats.at[p], send.at[k], recv.at[p], to).wait_recv()
            return c

        lax.fori_loop(1, n, wait, 0)
        total = jnp.sum(stats[...], axis=0)
        both = jnp.concatenate(
            [
                jnp.broadcast_to(total[:, :chans], (8, chans)),
                jnp.broadcast_to(total[:, chans:], (8, chans)),
            ],
            axis=0,
        )
        size = chans // GROUPS
        gi = lax.broadcasted_iota(jnp.int32, (chans, chans), 0) // size
        gj = lax.broadcasted_iota(jnp.int32, (chans, chans), 1) // size
        same = (gi == gj).astype(F32)
        sums = jnp.dot(both, same, preferred_element_type=F32, precision=lax.Precision.HIGHEST)
        count = float(size * bins * frames * n)
        mean = sums[0:1] / count
        var = sums[8:9] / count - mean * mean
        return mean, lax.rsqrt(var + EPSILON)

    def end_stats(stats, send, recv):
        def wait(k, c):
            p, to = peer_of(k)
            remote(stats.at[me], stats.at[me], send.at[k], recv.at[me], to).wait_send()
            return c

        lax.fori_loop(1, n, wait, 0)

    send_stats(s, q, stats1, s1_send, s1_recv)

    p_row = proj[...]
    hi, mid, low = [x.astype(F32) for x in three_parts(p_row)]
    row = lax.broadcasted_iota(jnp.int32, (16, chans), 0)
    parts = jnp.where(row == 0, hi, jnp.where(row == 1, mid, jnp.where(row == 2, low, 0.0))).astype(BF16)
    row24 = lax.broadcasted_iota(jnp.int32, (32, chans), 0)
    taps = jnp.zeros((32, chans), F32)
    for i in range(3):
        for j in range(3):
            wv = jnp.sum(dot_nt(parts, w2[3 * i + j]), axis=0, keepdims=True)
            a, b, _ = three_parts(wv)
            taps = jnp.where(row24 == 8 * j + i, a.astype(F32), taps)
            taps = jnp.where(row24 == 8 * j + 3 + i, b.astype(F32), taps)
    taps = taps.astype(BF16)
    direct = jnp.where(row24 == 9, hi, jnp.where(row24 == 12, mid, jnp.where(row24 == 14, low, 0.0))).astype(BF16)
    const = jnp.sum(p_row * bias2[...], axis=1, keepdims=True)

    h_bin.wait()

    @pl.when(has_left)
    def _():
        for c in go_left:
            c.wait_send()
        for c in go_right:
            c.wait_recv()

    @pl.when(has_right)
    def _():
        for c in go_right:
            c.wait_send()
        for c in go_left:
            c.wait_recv()

    mean, inv = take_stats(stats1, s1_send, s1_recv)
    scale = inv * gain1[...]
    shift = shift1[...]

    def silu(x, mean, scale, shift):
        y = (x - mean) * scale + shift
        h = 0.5 * y
        return h + h * jnp.tanh(h)

    left_on = jnp.where(has_left, 1.0, 0.0).astype(F32)
    right_on = jnp.where(has_right, 1.0, 0.0).astype(F32)

    def edge_act(ref, present):
        x = ref[...].astype(F32)
        return jnp.where(present, silu(x, mean, scale, shift), 0.0)

    act_l[...] = edge_act(halo_l, has_left)
    act_r[...] = edge_act(halo_r, has_right)
    cl = edge_act(corner_l, has_left)
    cr = edge_act(corner_r, has_right)
    pick = f * 15
    r16 = lax.broadcasted_iota(jnp.int32, (16, chans), 0)
    cl = jnp.sum(jnp.where(r16 == pick, cl, 0.0), axis=0, keepdims=True)
    cr = jnp.sum(jnp.where(r16 == pick, cr, 0.0), axis=0, keepdims=True)
    rows = lax.broadcasted_iota(jnp.int32, (frames, chans), 0)

    def put(at, x, left, right):
        spread[at, :, 0:chans] = jnp.where(rows == 0, left, pltpu.roll(x, 1, 0)).astype(BF16)
        spread[at, :, chans : 2 * chans] = x.astype(BF16)
        spread[at, :, 2 * chans : 3 * chans] = jnp.where(
            rows == frames - 1, right, pltpu.roll(x, frames - 1, 0)
        ).astype(BF16)

    put((1 - f) * (bins + 1), silu(halo_b[...].astype(F32), mean, scale, shift), cl, cr)
    spread[f * (bins + 1)] = jnp.zeros(spread.shape[1:], BF16)

    def norm_step(b, c):
        for u in range(4):
            at = b * 4 + u
            x = silu(lat[at].astype(F32), mean, scale, shift)
            put(at + 1, x, act_l[pl.ds(at, 1), :], act_r[pl.ds(at, 1), :])
        return c

    lax.fori_loop(0, bins // 4, norm_step, 0)

    nb = 8
    moved = tshift[...]

    def conv_step(b, carry):
        s, q = carry
        acc = jnp.zeros((nb * frames, chans), F32)
        for i in range(3):
            part = spread[pl.ds(b * nb + i, nb)].reshape(nb * frames, 3 * chans)
            acc = acc + dot(part, w1[i])
        out = (acc + moved).astype(BF16)
        first[pl.ds(b * nb, nb)] = out.reshape(nb, frames, chans)
        x = out.astype(F32)
        return s + fold(x), q + fold(x * x)

    s, q = lax.fori_loop(0, bins // nb, conv_step, (zero8, zero8))
    end_stats(stats1, s1_send, s1_recv)
    send_stats(s, q, stats2, s2_send, s2_recv)

    gpad[...] = jnp.zeros(gpad.shape, F32)
    mean2, inv2 = take_stats(stats2, s2_send, s2_recv)
    scale2 = inv2 * gain2[...]
    low2 = shift2[...]
    vb = 4
    sub = lax.broadcasted_iota(jnp.int32, (8, frames), 0)

    def tap_step(b, c):
        x = first[pl.ds(b * vb, vb)].reshape(vb * frames, chans).astype(F32)
        act = silu(x, mean2, scale2, low2).astype(BF16)
        raw = lat[pl.ds(b * vb, vb)].reshape(vb * frames, chans)
        g = dot_nt(taps, act) + dot_nt(direct, raw)
        for u in range(vb):
            at = b * vb + u
            own = mel[pl.ds(at, 1), :] * (1.0 / STEP_SIZE) + const
            for j in range(3):
                piece = g[8 * j : 8 * j + 8, u * frames : (u + 1) * frames]
                if j == 1:
                    piece = jnp.where(sub == 7, own, piece)
                gpad[j, at + 2, :, 0:frames] = piece
        return c

    lax.fori_loop(0, bins // vb, tap_step, 0)
    end_stats(stats2, s2_send, s2_recv)

    tall = bins + 8
    subs = lax.broadcasted_iota(jnp.int32, (tall, 8, 128), 1)
    total = jnp.zeros((tall, 128), F32)
    for j in range(3):
        comb = jnp.zeros((tall, 8, 128), F32)
        for i in range(3):
            mine = (subs == i) | (subs == i + 3)
            if i == 1:
                mine = mine | (subs >= 6)
            comb = jnp.where(mine, gpad[j, i : i + tall], comb)
        rowsum = jnp.sum(comb, axis=1)
        total = total + (pltpu.roll(rowsum, 2 - j, 1) if j < 2 else rowsum)
    z = jnp.concatenate([total * STEP_SIZE, jnp.zeros((128 - tall, 128), F32)], axis=0)
    wide = frames + 8
    zt[...] = jnp.transpose(z)[0:wide]

    top = frames - 8
    z_own = remote(zt, z_part, z_send.at[0], z_recv.at[0], partner)
    z_left = [
        remote(zt.at[pl.ds(0, 8)], z_after.at[0], z_send.at[1], z_recv.at[1], to_left[0]),
        remote(zt.at[pl.ds(0, 8)], z_after.at[1], z_send.at[2], z_recv.at[2], to_left[1]),
    ]
    z_right = [
        remote(zt.at[pl.ds(top, 16)], z_before.at[0], z_send.at[3], z_recv.at[3], to_right[0]),
        remote(zt.at[pl.ds(top, 16)], z_before.at[1], z_send.at[4], z_recv.at[4], to_right[1]),
    ]

    @pl.when(has_left)
    def _():
        for c in z_left:
            c.start()

    @pl.when(has_right)
    def _():
        for c in z_right:
            c.start()

    z_own.start()

    @pl.when(has_left)
    def _():
        for c in z_left:
            c.wait_send()
        for c in z_right:
            c.wait_recv()

    @pl.when(has_right)
    def _():
        for c in z_right:
            c.wait_send()
        for c in z_left:
            c.wait_recv()

    z_own.wait()

    def lane_place(mine, theirs):
        shape = mine.shape
        lane = lax.broadcasted_iota(jnp.int32, shape, 1)
        low = jnp.where(f == 0, mine, theirs)
        high = jnp.where(f == 0, theirs, mine)
        low = jnp.where(lane <= bins, pltpu.roll(low, 127, 1), 0.0)
        high = jnp.where(lane >= bins - 1, pltpu.roll(high, bins - 1, 1), 0.0)
        return low + high

    span = frames + 16
    center = lane_place(zt[...], z_part[...])
    before = jnp.where(has_left, lane_place(z_before[0], z_before[1]), 0.0)
    after = jnp.where(has_right, lane_place(z_after[0], z_after[1]), 0.0)
    big = jnp.concatenate([center, jnp.zeros((8, 128), F32)], axis=0)
    big = pltpu.roll(big, 7, 0)
    r_b = lax.broadcasted_iota(jnp.int32, (16, 128), 0)
    before = jnp.where(r_b >= 1, before, 0.0)
    before = jnp.concatenate([before, jnp.zeros((span - 16, 128), F32)], axis=0)
    before = pltpu.roll(before, span - 1, 0)
    after = jnp.concatenate([after, jnp.zeros((span - 8, 128), F32)], axis=0)
    after = pltpu.roll(after, frames + 7, 0)
    pos = lax.broadcasted_iota(jnp.int32, (span, 128), 0) - 8 + tm * frames
    whole = jnp.where((pos >= 0) & (pos < n_tm * frames), big + before + after, 0.0)
    mt_out[...] = whole.astype(BF16)
    turned[...] = jnp.transpose(
        jnp.concatenate([whole[8 : 8 + frames], jnp.zeros((128 - frames, 128), F32)], axis=0)
    )
    mel_out[...] = turned[pl.ds(pl.multiple_of(f * bins, 8), bins), 0:frames]


def up_kernel(
    n_tm, frames,
    mt, pre, pre_bias, up, up_bias, out, taps_in, spread, acc,
):
    step = pl.program_id(0)
    span, bins = mt.shape
    n_taps, block, _ = pre.shape
    kernel_taps = up.shape[0] // block
    tm = lax.axis_index("tm")

    @pl.when(step == 0)
    def _():
        m = mt[...].astype(F32)
        for k in range(n_taps):
            s = (n_taps // 2 - k) % span
            taps_in[:, k * bins : (k + 1) * bins] = (pltpu.roll(m, s, 0) if s else m).astype(BF16)
        r = lax.broadcasted_iota(jnp.int32, spread.shape, 0)
        c = lax.broadcasted_iota(jnp.int32, spread.shape, 1)
        spread[...] = (c // kernel_taps == r).astype(F32).astype(BF16)
        acc[...] = jnp.zeros(acc.shape, F32)

    total = jnp.zeros((span, block), F32)
    for k in range(n_taps):
        total = total + dot_nt(taps_in[:, k * bins : (k + 1) * bins], pre[k])
    pos = lax.broadcasted_iota(jnp.int32, (span, block), 0) - 8 + tm * frames
    feats = jnp.where((pos >= 0) & (pos < n_tm * frames), total + pre_bias[...], 0.0).astype(BF16)
    wide = dot(feats, spread[...])
    lane = lax.broadcasted_iota(jnp.int32, wide.shape, 1)
    tap = lax.rem(lane, kernel_taps)
    wide = jnp.where(tap < 4, wide, pltpu.roll(wide, 1, 0))
    phase = lax.rem(lane[0:frames], 4)
    pieces = []
    for p in range(4):
        start = 8 + (1 if p >= 2 else 0)
        pieces.append(jnp.where(phase == (p + 2) % 4, wide[start : start + frames], 0.0).astype(BF16))
    acc[...] += dot(jnp.concatenate(pieces, axis=0), up[...])

    @pl.when(step == pl.num_programs(0) - 1)
    def _():
        rows = acc.shape[0]
        done = (acc[...] + up_bias[...]).astype(BF16).astype(F32)
        r = lax.broadcasted_iota(jnp.int32, (rows, rows), 0)
        c = lax.broadcasted_iota(jnp.int32, (rows, rows), 1)
        perm = (r == lax.rem(c, 4) * frames + c // 4).astype(F32).astype(BF16)
        out[...] = dot(jnp.transpose(done).astype(BF16), perm).astype(BF16)


def shards(
    latent, mel_noisy, time_shift, first_gain, first_shift, conv_first, second_gain,
    second_shift, conv_second, second_bias, out_proj, pre_weight, pre_bias, up_weight, up_bias,
):
    chans, bins, frames = latent.shape
    n_tm, n_f = lax.axis_size("tm"), lax.axis_size("freq")
    n = n_tm * n_f
    lat = jnp.transpose(latent, (1, 2, 0))
    pre_full = lax.all_gather(jnp.transpose(pre_weight, (1, 0, 2)), "tm", axis=1, tiled=True)
    vec = lambda v: v.reshape(1, -1)
    vmem = pl.BlockSpec(memory_space=pltpu.VMEM)
    span = frames + 16
    dma = pltpu.SemaphoreType.DMA
    mel_next, mt = pl.pallas_call(
        functools.partial(block_kernel, n_tm, n_f),
        out_shape=(
            jax.ShapeDtypeStruct((bins, frames), F32),
            jax.ShapeDtypeStruct((span, 128), BF16),
        ),
        in_specs=[vmem] * 11,
        out_specs=(vmem, vmem),
        scratch_shapes=[
            pltpu.VMEM((n, 1, 2 * chans), F32),
            pltpu.VMEM((n, 1, 2 * chans), F32),
            pltpu.VMEM((bins, chans), BF16),
            pltpu.VMEM((bins, chans), BF16),
            pltpu.VMEM((bins, chans), BF16),
            pltpu.VMEM((bins, chans), BF16),
            pltpu.VMEM((frames, chans), BF16),
            pltpu.VMEM((16, chans), BF16),
            pltpu.VMEM((16, chans), BF16),
            pltpu.VMEM((bins, chans), F32),
            pltpu.VMEM((bins, chans), F32),
            pltpu.VMEM((bins + 2, frames, 3 * chans), BF16),
            pltpu.VMEM((bins, frames, chans), BF16),
            pltpu.VMEM((3, bins + 16, 8, 128), F32),
            pltpu.VMEM((frames + 8, 128), F32),
            pltpu.VMEM((frames + 8, 128), F32),
            pltpu.VMEM((2, 16, 128), F32),
            pltpu.VMEM((2, 8, 128), F32),
            pltpu.VMEM((128, 128), F32),
            dma((n,)), dma((n,)), dma((n,)), dma((n,)),
            dma((5,)), dma((5,)), dma((5,)), dma((5,)),
        ],
        compiler_params=pltpu.CompilerParams(
            collective_id=0, has_side_effects=True, vmem_limit_bytes=40 * 2**20
        ),
        cost_estimate=pl.CostEstimate(
            flops=2 * 9 * bins * frames * chans * chans, bytes_accessed=5 * 2**20, transcendentals=0
        ),
    )(
        lat, mel_noisy, vec(time_shift), vec(first_gain), vec(first_shift),
        conv_first.reshape(3, 3 * chans, chans), vec(second_gain), vec(second_shift),
        conv_second.reshape(9, chans, chans), vec(second_bias), vec(out_proj),
    )

    n_taps, width, mels = pre_full.shape
    k_taps, outs = up_weight.shape[1], up_weight.shape[2]
    block = 256
    vocal = pl.pallas_call(
        functools.partial(up_kernel, n_tm, frames),
        grid=(width // block,),
        out_shape=jax.ShapeDtypeStruct((outs, 4 * frames), BF16),
        in_specs=[
            pl.BlockSpec((span, mels), lambda i: (0, 0)),
            pl.BlockSpec((n_taps, block, mels), lambda i: (0, i, 0)),
            pl.BlockSpec((1, block), lambda i: (0, i)),
            pl.BlockSpec((block * k_taps, outs), lambda i: (i, 0)),
            pl.BlockSpec((1, outs), lambda i: (0, 0)),
        ],
        out_specs=pl.BlockSpec((outs, 4 * frames), lambda i: (0, 0)),
        scratch_shapes=[
            pltpu.VMEM((span, n_taps * mels), BF16),
            pltpu.VMEM((block, block * k_taps), BF16),
            pltpu.VMEM((4 * frames, outs), F32),
        ],
        compiler_params=pltpu.CompilerParams(vmem_limit_bytes=40 * 2**20),
        cost_estimate=pl.CostEstimate(
            flops=2 * 4 * frames * width * k_taps * outs, bytes_accessed=13 * 2**20, transcendentals=0
        ),
    )(mt, pre_full, vec(pre_bias), up_weight.reshape(width * k_taps, outs), vec(up_bias))
    return (mel_next, vocal)


def solution(mesh):
    in_specs = (
        P(None, "freq", ("song", "tm")),
        P("freq", ("song", "tm")),
        P("song"),
        P(),
        P(),
        P(),
        P(),
        P(),
        P(),
        P(),
        P(),
        P("tm", None, None),
        P(),
        P(None, None, "freq"),
        P("freq"),
    )
    out_specs = (P("freq", ("song", "tm")), P("freq", ("song", "tm")))
    return jax.shard_map(shards, mesh=mesh, in_specs=in_specs, out_specs=out_specs, check_vma=False)
```

time: 245 us -> 93.2 us (0.38)
  matrix products: 76.5 us -> 0 us
  blocking collectives: 70.9 us -> 0 us
  Pallas kernels: 0 us -> 42.7 us
  local copies, waits for them, and re-layouts: 49.7 us -> 15.7 us
  waiting for transfers between devices: 4.92 us -> 20.1 us
  other arithmetic: 14.3 us -> 0 us
  starting transfers between devices: 13.8 us -> 0.04 us
    dot_general x33 -> x0, matrix products: 76.5 us -> none  [the longest x18 63.5 us: conv_valid(): jnp.einsum('io,ift->oft', weight[i, j], padded[:, i:i + bins, j:j + frame...]
    psum x2 -> x0, blocking collectives: 68.3 us -> none  [group_moments(): first, second = lax.psum((first, second), ('tm', 'freq'))]
    slice x4 -> x0, local copies, waits for them, and re-layouts: 44.5 us -> none  [the longest x1 44.2 us: up_tap(): up_weight[:, k, :]]
    pallas_call x0 -> x2, Pallas kernels: none -> 42.7 us  [the longest x1 33.2 us: shards(): pl.pallas_call(functools.partial(block_kernel, n_tm, n_f), out_shape=(jax...]
    all_gather x1, waiting for transfers between devices: 0.01 us -> 19.5 us  [shards(): lax.all_gather(jnp.transpose(pre_weight, (1, 0, 2)), 'tm', axis=1, tiled=...]
    ppermute x10 -> x0, starting transfers between devices: 13.7 us -> none  [the longest x5 6.99 us: padded_2(): after = lax.ppermute(first, axis, down)]
    unnamed x35 -> x31, local copies, waits for them, and re-layouts: 3.86 us -> 15.7 us
    convert_element_type x4 -> x0, other arithmetic: 5.9 us -> none  [the longest x2 4.49 us: norm_silu(): apply_norm(values_in, mean, scale_inv, gain, shift).astype(jnp.bfloat16)]
  transfers between devices with their start and end apart: 11 -> 1, of which waited for: 3 -> 1; matrix products, arithmetic and copies ran while one was open for 49% -> 0% of each run, Pallas kernels for 0% -> 36%
where the time goes in v1:
time: 93.2 us; the launch traced here: 92.7 us
  Pallas kernels  42.7 us (46%)
  waiting for transfers between devices  20.1 us (22%)
  local copies, waits for them, and re-layouts  15.7 us (17%)
  between operations  14.1 us (15%)
    pallas_call x1, Pallas kernels, shards(): pl.pallas_call(functools.partial(block_kernel, n_tm, n_f), out_shape=(jax...  33.2 us
    all_gather x1, waiting for transfers between devices, shards(): lax.all_gather(jnp.transpose(pre_weight, (1, 0, 2)), 'tm', axis=1, tiled=...  19.5 us
    unnamed x31, local copies, waits for them, and re-layouts  15.7 us
    pallas_call x1, Pallas kernels, shards(): pl.pallas_call(functools.partial(up_kernel, n_tm, frames), grid=(width //...  9.47 us
  transfers between devices with their start and end apart: 1, of which 1 were waited for; matrix products, arithmetic and copies ran while one was open for 0% of the time, Pallas kernels for 36%

profile of v1, /device:TPU:0, one launch (start us, length us, event | category | flops | bytes accessed | tf_op | source)
XLA Modules:
  0.0 92.7 jit_solution(8508381676845083752)
XLA Ops:
  7.2 0.0 all-gather.2.cloned.1.call-start
  7.2 0.7 all-gather.2.cloned.1.call-update
  7.9 0.0 copy-start.2
  7.9 1.6 %copy-done.2 = bf16[256,64,64]{0,2,1:T(8,128)(2,1)S(1)} copy-done((bf16[256,64,64]{0,2,1:T(8,128)(2,1)S(1)}, bf16[256,64,64]{0,2,1:T(8,128)(2,1)}, u32[]{:S(2)}) %copy-start.2) | copy-done | bytes 2097176
  9.5 0.0 copy-start.3
  9.5 1.3 %copy-done.3 = bf16[3,3,256,256]{3,2,1,0:T(8,128)(2,1)S(1)} copy-done((bf16[3,3,256,256]{3,2,1,0:T(8,128)(2,1)S(1)}, bf16[3,3,256,256]{3,2,1,0:T(8,128)(2,1)}, u32[]{:S(2)}) %copy-start.3) | copy-done | bytes 1179672
  10.8 0.0 copy-start.4
  10.8 1.3 %copy-done.4 = bf16[3,3,256,256]{3,2,1,0:T(8,128)(2,1)S(1)} copy-done((bf16[3,3,256,256]{3,2,1,0:T(8,128)(2,1)S(1)}, bf16[3,3,256,256]{3,2,1,0:T(8,128)(2,1)}, u32[]{:S(2)}) %copy-start.4) | copy-done | bytes 1179672
  12.0 0.0 copy-start.5
  12.0 0.8 copy-done.5
  12.8 0.0 copy-start.6
  12.8 0.7 copy-done.6
  13.5 0.0 copy-start.7
  13.5 0.7 copy-done.7
  14.2 0.0 copy-start.8
  14.2 0.7 copy-done.8
  14.8 0.0 copy-start.9
  14.8 0.7 copy-done.9
  15.5 0.0 copy-start.10
  15.5 0.7 copy-done.10
  16.2 0.0 copy-start.11
  16.2 0.7 copy-done.11
  16.9 0.0 copy-start.12
  16.9 0.7 copy-done.12
  17.6 0.0 copy-start.13
  17.6 0.0 copy-start.14
  17.6 33.2 %shard_map.158 = (f32[64,64]{1,0:T(8,128)S(1)}, bf16[80,128]{1,0:T(8,128)(2,1)S(1)}) custom-call(bf16[64,64,256]{2,1,0:T(8,128)(2,1)S(1)} %bitcast.13, f32[64,64]{1,0:T(8,128)S(1)} %copy-done.5, f32[1,256]{1,0:T(1,128)S(1)} %bitcast.16, f32[1,256]{1,0:T(1,128)S(1)} %bitcast.17, f32[1,256]{1,0:T(1,128)S(1)} %bitcast.18, bf16[3,768,256]{2,1,0:T(8,128)(2,1)S(1)} %bitcast.14, ...), custom_call_target="tpu_custom_call" | custom-call | flops 4831838208 | bytes 5242880 | tf_op jit(solution)/shard_map/pallas_call | solution.py:425
  50.8 0.0 copy-done.13
  50.8 0.0 copy-done.14
  50.8 19.5 %all-gather.2.cloned.1.call-done.pre = bf16[7,1536,128]{2,1,0:T(8,128)(2,1)} async-done(((bf16[7,192,128]{2,1,0:T(8,128)(2,1)}), bf16[7,1536,128]{2,1,0:T(8,128)(2,1)}) %all-gather.2.cloned.1.call-update) | async-done | bytes 2752528 | tf_op jit(solution)/shard_map/all_gather | solution.py:420
  70.3 0.0 copy-start
  70.3 3.7 %copy-done = bf16[1536,8,384]{2,1,0:T(8,128)(2,1)S(1)} copy-done((bf16[1536,8,384]{2,1,0:T(8,128)(2,1)S(1)}, bf16[1536,8,384]{2,1,0:T(8,128)(2,1)}, u32[]{:S(2)}) %copy-start) | copy-done | bytes 9437208
  74.0 0.0 copy-start.1
  74.0 1.8 %copy-done.1 = bf16[7,1536,128]{2,1,0:T(8,128)(2,1)S(1)} copy-done((bf16[7,1536,128]{2,1,0:T(8,128)(2,1)S(1)}, bf16[7,1536,128]{2,1,0:T(8,128)(2,1)}, u32[]{:S(2)}) %copy-start.1) | copy-done | bytes 2752536
  75.8 9.5 %shard_map.159 = bf16[384,256]{1,0:T(8,128)(2,1)} custom-call(bf16[80,128]{1,0:T(8,128)(2,1)S(1)} %get-tuple-element.5.mt, bf16[7,1536,128]{2,1,0:T(8,128)(2,1)S(1)} %copy-done.1, f32[1,1536]{1,0:T(1,128)S(1)} %reshape.49.pre_bias, bf16[12288,384]{1,0:T(8,128)(2,1)S(1)} %bitcast.12, f32[1,384]{1,0:T(1,128)S(1)} %reshape.51.up_bias), custom_call_target="tpu_custom_call" | custom-call | flops 2415919104 | bytes 13631488 | tf_op jit(solution)/shard_map/pallas_call | solution.py:471
  85.2 0.6 copy.18
  (2 shorter events, 0.0 us)
Async XLA Ops:
  7.2 63.1 %all-gather.2.cloned.1.call-start = ((), (), s32[]{:S(2)}) async-start(), calls=%async_computation | async-start | bytes 3096576 | tf_op jit(solution)/shard_map/all_gather | solution.py:420
  7.9 1.6 %copy-start.2 = (bf16[256,64,64]{0,2,1:T(8,128)(2,1)S(1)}, bf16[256,64,64]{0,2,1:T(8,128)(2,1)}, u32[]{:S(2)}) copy-start(bf16[256,64,64]{0,2,1:T(8,128)(2,1)} %param.15) | copy-start | bytes 6291460
  9.5 1.3 %copy-start.3 = (bf16[3,3,256,256]{3,2,1,0:T(8,128)(2,1)S(1)}, bf16[3,3,256,256]{3,2,1,0:T(8,128)(2,1)}, u32[]{:S(2)}) copy-start(bf16[3,3,256,256]{3,2,1,0:T(8,128)(2,1)} %param.20) | copy-start | bytes 3538948
  10.8 1.3 %copy-start.4 = (bf16[3,3,256,256]{3,2,1,0:T(8,128)(2,1)S(1)}, bf16[3,3,256,256]{3,2,1,0:T(8,128)(2,1)}, u32[]{:S(2)}) copy-start(bf16[3,3,256,256]{3,2,1,0:T(8,128)(2,1)} %param.23) | copy-start | bytes 3538948
  12.0 0.8 copy-start.5
  12.8 0.7 copy-start.6
  13.5 0.7 copy-start.7
  14.2 0.7 copy-start.8
  14.8 0.7 copy-start.9
  15.5 0.7 copy-start.10
  16.2 0.7 copy-start.11
  16.9 0.7 copy-start.12
  17.6 33.2 %copy-start.13 = (f32[1536]{0:T(1024)S(1)}, f32[1536]{0:T(1024)}, u32[]{:S(2)}) copy-start(f32[1536]{0:T(1024)} %param.27) | copy-start | bytes 18436
  17.6 33.3 %copy-start.14 = (f32[384]{0:T(512)S(1)}, f32[384]{0:T(512)}, u32[]{:S(2)}) copy-start(f32[384]{0:T(512)} %param.29) | copy-start | bytes 4612
  70.3 3.7 %copy-start = (bf16[1536,8,384]{2,1,0:T(8,128)(2,1)S(1)}, bf16[1536,8,384]{2,1,0:T(8,128)(2,1)}, u32[]{:S(2)}) copy-start(bf16[1536,8,384]{2,1,0:T(8,128)(2,1)} %param.28) | copy-start | bytes 28311556
  74.0 1.8 %copy-start.1 = (bf16[7,1536,128]{2,1,0:T(8,128)(2,1)S(1)}, bf16[7,1536,128]{2,1,0:T(8,128)(2,1)}, u32[]{:S(2)}) copy-start(bf16[7,1536,128]{2,1,0:T(8,128)(2,1)} %all-gather.2.cloned.1.call-done.pre) | copy-start | bytes 8257540
Sparse Core Ops, SparseCore 0:
  10.2 60.0 all-gather.1

commit v2 on v1

--- a/solution.py
+++ b/solution.py
@@ -33,12 +33,18 @@
 
 
 def block_kernel(
-    n_tm, n_f,
-    lat, mel, tshift, gain1, shift1, w1, gain2, shift2, w2, bias2, proj,
-    mel_out, mt_out,
+    n_tm, n_f, fused,
+    lat_h, mel_h, tshift_h, gain1_h, shift1_h, w1_h, gain2_h, shift2_h, w2_h, bias2_h, proj_h,
+    pre_h, pre_bias_h, up_h, up_bias_h,
+    mel_out, vocal,
+    lat, mel, tshift, gain1, shift1, w1, gain2, shift2, w2, bias2, proj, pre_bias, up_bias,
+    pre, up,
     stats1, stats2, stage_l, stage_r, halo_l, halo_r, halo_b, corner_l, corner_r,
     act_l, act_r, spread, first, gpad, zt, z_part, z_before, z_after, turned,
+    taps_in, repeat, feats, wide_f, acc,
+    in_sem, up_sem, own_sem,
     s1_send, s1_recv, s2_send, s2_recv, h_send, h_recv, z_send, z_recv,
+    p_send, p_recv, fw_send, ft_send, ft_recv,
 ):
     bins, frames, chans = lat.shape
     n = n_tm * n_f
@@ -54,12 +60,25 @@
         return p, {"tm": p // n_f, "freq": lax.rem(p, n_f)}
 
     barrier = pltpu.get_barrier_semaphore()
+    loads = [
+        pltpu.make_async_copy(src, dst, in_sem.at[i])
+        for i, (src, dst) in enumerate([
+            (lat_h, lat), (w2_h, w2), (w1_h, w1), (mel_h, mel), (tshift_h, tshift), (gain1_h, gain1),
+            (shift1_h, shift1), (gain2_h, gain2), (shift2_h, shift2), (bias2_h, bias2), (proj_h, proj),
+            (pre_bias_h, pre_bias), (up_bias_h, up_bias),
+        ])
+    ]
 
     def greet(k, c):
         pl.semaphore_signal(barrier, inc=1, device_id=peer_of(k)[1], device_id_type=MESH)
         return c
 
     lax.fori_loop(1, n, greet, 0)
+    for c in loads:
+        c.start()
+    loads[0].wait()
+    load_up = pltpu.make_async_copy(up_h, up, up_sem)
+    load_up.start()
 
     sub8 = lax.broadcasted_iota(jnp.int32, (bins, 8, chans), 1)
     head = lat[:, 0:16, :].astype(F32)[:, 0:8, :]
@@ -157,6 +176,86 @@
 
     send_stats(s, q, stats1, s1_send, s1_recv)
 
+    half_n = n_tm // n_f
+    slot = lax.rem(tm, half_n)
+    beside = tm + 1 - 2 * lax.rem(tm, 2)
+    holder = f == tm // half_n
+
+    def push(k):
+        to = jnp.where(k == 0, beside, lax.rem(tm + 2 * k, n_tm))
+        return remote(pre_h, pre.at[:, slot], p_send.at[k], p_recv.at[slot], {"tm": to, "freq": f})
+
+    def forward(j):
+        d = 2 * j + lax.rem(tm, 2)
+        return d, remote(pre.at[:, d], pre.at[:, d], fw_send.at[j], p_recv.at[d], {"tm": beside, "freq": f})
+
+    if fused:
+        own_pre = pltpu.make_async_copy(pre_h, pre.at[:, slot], own_sem)
+    else:
+        own_pre = pltpu.make_async_copy(pre_h, pre, own_sem)
+        own_pre.start()
+
+    def gather_start():
+        @pl.when(holder)
+        def _():
+            own_pre.start()
+
+            def go(k, c):
+                push(k).start()
+                return c
+
+            lax.fori_loop(0, n_tm // 2, go, 0)
+
+    def gather_forward():
+        def go(j, c):
+            d, copy = forward(j)
+
+            @pl.when(d + f * half_n != tm)
+            def _():
+                copy.wait_recv()
+                copy.start()
+
+            return c
+
+        lax.fori_loop(0, half_n // 2, go, 0)
+
+    def gather_end():
+        @pl.when(holder)
+        def _():
+            own_pre.wait()
+
+            def wait(k, c):
+                push(k).wait_send()
+                return c
+
+            lax.fori_loop(0, n_tm // 2, wait, 0)
+
+        def rest(j, c):
+            d, copy = forward(j)
+
+            @pl.when(d + f * half_n != tm)
+            def _():
+                copy.wait_send()
+
+            e = 2 * j + 1 - lax.rem(tm, 2)
+            remote(pre.at[:, e], pre.at[:, e], fw_send.at[j], p_recv.at[e], {"tm": beside, "freq": f}).wait_recv()
+            return c
+
+        lax.fori_loop(0, half_n // 2, rest, 0)
+
+    if fused:
+        gather_start()
+
+    for c in loads[1:]:
+        c.wait()
+
+    k_taps = repeat.shape[1] // 128
+    r = lax.broadcasted_iota(jnp.int32, repeat.shape, 0)
+    c = lax.broadcasted_iota(jnp.int32, repeat.shape, 1)
+    repeat[...] = (c // k_taps == r).astype(F32).astype(BF16)
+    acc[...] = jnp.zeros(acc.shape, F32)
+    gpad[...] = jnp.zeros(gpad.shape, F32)
+
     p_row = proj[...]
     hi, mid, low = [x.astype(F32) for x in three_parts(p_row)]
     row = lax.broadcasted_iota(jnp.int32, (16, chans), 0)
@@ -252,7 +351,8 @@
     end_stats(stats1, s1_send, s1_recv)
     send_stats(s, q, stats2, s2_send, s2_recv)
 
-    gpad[...] = jnp.zeros(gpad.shape, F32)
+    if fused:
+        gather_forward()
     mean2, inv2 = take_stats(stats2, s2_send, s2_recv)
     scale2 = inv2 * gain2[...]
     low2 = shift2[...]
@@ -355,58 +455,59 @@
     after = pltpu.roll(after, frames + 7, 0)
     pos = lax.broadcasted_iota(jnp.int32, (span, 128), 0) - 8 + tm * frames
     whole = jnp.where((pos >= 0) & (pos < n_tm * frames), big + before + after, 0.0)
-    mt_out[...] = whole.astype(BF16)
     turned[...] = jnp.transpose(
         jnp.concatenate([whole[8 : 8 + frames], jnp.zeros((128 - frames, 128), F32)], axis=0)
     )
     mel_out[...] = turned[pl.ds(pl.multiple_of(f * bins, 8), bins), 0:frames]
 
-
-def up_kernel(
-    n_tm, frames,
-    mt, pre, pre_bias, up, up_bias, out, taps_in, spread, acc,
-):
-    step = pl.program_id(0)
-    span, bins = mt.shape
-    n_taps, block, _ = pre.shape
-    kernel_taps = up.shape[0] // block
-    tm = lax.axis_index("tm")
-
-    @pl.when(step == 0)
-    def _():
-        m = mt[...].astype(F32)
-        for k in range(n_taps):
-            s = (n_taps // 2 - k) % span
-            taps_in[:, k * bins : (k + 1) * bins] = (pltpu.roll(m, s, 0) if s else m).astype(BF16)
-        r = lax.broadcasted_iota(jnp.int32, spread.shape, 0)
-        c = lax.broadcasted_iota(jnp.int32, spread.shape, 1)
-        spread[...] = (c // kernel_taps == r).astype(F32).astype(BF16)
-        acc[...] = jnp.zeros(acc.shape, F32)
-
-    total = jnp.zeros((span, block), F32)
+    m = whole.astype(BF16).astype(F32)
+    n_taps, mels = pre.shape[0], pre.shape[-1]
+    width = feats.shape[2]
     for k in range(n_taps):
-        total = total + dot_nt(taps_in[:, k * bins : (k + 1) * bins], pre[k])
-    pos = lax.broadcasted_iota(jnp.int32, (span, block), 0) - 8 + tm * frames
-    feats = jnp.where((pos >= 0) & (pos < n_tm * frames), total + pre_bias[...], 0.0).astype(BF16)
-    wide = dot(feats, spread[...])
-    lane = lax.broadcasted_iota(jnp.int32, wide.shape, 1)
-    tap = lax.rem(lane, kernel_taps)
-    wide = jnp.where(tap < 4, wide, pltpu.roll(wide, 1, 0))
+        s = (n_taps // 2 - k) % span
+        taps_in[:, k * mels : (k + 1) * mels] = (pltpu.roll(m, s, 0) if s else m).astype(BF16)
+    if fused:
+        gather_end()
+    else:
+        own_pre.wait()
+    made = jnp.zeros((span, width), F32)
+    for k in range(n_taps):
+        made = made + dot_nt(taps_in[:, k * mels : (k + 1) * mels], pre[k].reshape(width, mels))
+    pos = lax.broadcasted_iota(jnp.int32, (span, width), 0) - 8 + tm * frames
+    made = made + pre_bias[:, pl.ds(pl.multiple_of(f * width, 128), width)]
+    feats[f] = jnp.where((pos >= 0) & (pos < n_tm * frames), made, 0.0).astype(BF16)
+    swap = remote(feats.at[f], feats.at[f], ft_send, ft_recv, partner)
+    swap.start()
+    load_up.wait()
+
+    group = wide_f.shape[1] // k_taps
+    rep = 128 * k_taps
+    lane = lax.broadcasted_iota(jnp.int32, (span, rep), 1)
+    upper = lax.rem(lane, k_taps) < 4
     phase = lax.rem(lane[0:frames], 4)
-    pieces = []
-    for p in range(4):
-        start = 8 + (1 if p >= 2 else 0)
-        pieces.append(jnp.where(phase == (p + 2) % 4, wide[start : start + frames], 0.0).astype(BF16))
-    acc[...] += dot(jnp.concatenate(pieces, axis=0), up[...])
-
-    @pl.when(step == pl.num_programs(0) - 1)
-    def _():
-        rows = acc.shape[0]
-        done = (acc[...] + up_bias[...]).astype(BF16).astype(F32)
-        r = lax.broadcasted_iota(jnp.int32, (rows, rows), 0)
-        c = lax.broadcasted_iota(jnp.int32, (rows, rows), 1)
-        perm = (r == lax.rem(c, 4) * frames + c // 4).astype(F32).astype(BF16)
-        out[...] = dot(jnp.transpose(done).astype(BF16), perm).astype(BF16)
+
+    def upsample(h):
+        for g in range(width // group):
+            for t in range(group // 128):
+                at = g * group + t * 128
+                wide = dot(feats[h, :, at : at + 128], repeat[...])
+                wide = jnp.where(upper, wide, pltpu.roll(wide, 1, 0))
+                for p in range(4):
+                    start = 8 + (1 if p >= 2 else 0)
+                    wide_f[p * frames : (p + 1) * frames, t * rep : (t + 1) * rep] = jnp.where(
+                        phase == (p + 2) % 4, wide[start : start + frames], 0.0
+                    ).astype(BF16)
+            row = pl.multiple_of((h * width + g * group) * k_taps, 128)
+            acc[...] += dot(wide_f[...], up[pl.ds(row, group * k_taps), :])
+
+    upsample(f)
+    swap.wait()
+    upsample(other)
+    done = (acc[...] + up_bias[...]).astype(BF16).astype(F32)
+    r = lax.broadcasted_iota(jnp.int32, (4 * frames, 4 * frames), 0)
+    c = lax.broadcasted_iota(jnp.int32, (4 * frames, 4 * frames), 1)
+    perm = (r == lax.rem(c, 4) * frames + c // 4).astype(F32).astype(BF16)
+    vocal[...] = dot(jnp.transpose(done).astype(BF16), perm).astype(BF16)
 
 
 def shards(
@@ -417,20 +518,40 @@
     n_tm, n_f = lax.axis_size("tm"), lax.axis_size("freq")
     n = n_tm * n_f
     lat = jnp.transpose(latent, (1, 2, 0))
-    pre_full = lax.all_gather(jnp.transpose(pre_weight, (1, 0, 2)), "tm", axis=1, tiled=True)
     vec = lambda v: v.reshape(1, -1)
     vmem = pl.BlockSpec(memory_space=pltpu.VMEM)
+    hbm = pl.BlockSpec(memory_space=pl.ANY)
     span = frames + 16
     dma = pltpu.SemaphoreType.DMA
-    mel_next, mt = pl.pallas_call(
-        functools.partial(block_kernel, n_tm, n_f),
+    pre = jnp.transpose(pre_weight, (1, 0, 2))
+    n_taps, rows, mels = pre.shape
+    k_taps, outs = up_weight.shape[1], up_weight.shape[2]
+    half = n_tm * rows // n_f
+    fused = rows % 16 == 0 and n_tm % 4 == 0
+    if fused:
+        held = (n_taps, n_tm // n_f, rows, mels)
+    else:
+        held = (n_taps, half, mels)
+        pre = lax.all_gather(pre, "tm", axis=1, tiled=True)
+        pre = lax.dynamic_slice_in_dim(pre, lax.axis_index("freq") * half, half, axis=1)
+    operands = (
+        lat, mel_noisy, vec(time_shift), vec(first_gain), vec(first_shift),
+        conv_first.reshape(3, 3 * chans, chans), vec(second_gain), vec(second_shift),
+        conv_second.reshape(9, chans, chans), vec(second_bias), vec(out_proj),
+        pre, vec(pre_bias), up_weight.reshape(-1, outs), vec(up_bias),
+    )
+    copies = [pltpu.VMEM(x.shape, x.dtype) for x in operands[:11] + (operands[12], operands[14])]
+    return pl.pallas_call(
+        functools.partial(block_kernel, n_tm, n_f, fused),
         out_shape=(
             jax.ShapeDtypeStruct((bins, frames), F32),
-            jax.ShapeDtypeStruct((span, 128), BF16),
+            jax.ShapeDtypeStruct((outs, 4 * frames), BF16),
         ),
-        in_specs=[vmem] * 11,
+        in_specs=[hbm] * 15,
         out_specs=(vmem, vmem),
-        scratch_shapes=[
+        scratch_shapes=copies + [
+            pltpu.VMEM(held, BF16),
+            pltpu.VMEM(operands[13].shape, BF16),
             pltpu.VMEM((n, 1, 2 * chans), F32),
             pltpu.VMEM((n, 1, 2 * chans), F32),
             pltpu.VMEM((bins, chans), BF16),
@@ -450,47 +571,23 @@
             pltpu.VMEM((2, 16, 128), F32),
             pltpu.VMEM((2, 8, 128), F32),
             pltpu.VMEM((128, 128), F32),
+            pltpu.VMEM((span, n_taps * mels), BF16),
+            pltpu.VMEM((128, 128 * k_taps), BF16),
+            pltpu.VMEM((2, span, half), BF16),
+            pltpu.VMEM((4 * frames, 384 * k_taps), BF16),
+            pltpu.VMEM((4 * frames, outs), F32),
+            dma((13,)), dma, dma,
             dma((n,)), dma((n,)), dma((n,)), dma((n,)),
             dma((5,)), dma((5,)), dma((5,)), dma((5,)),
+            dma((n_tm,)), dma((n_tm,)), dma((n_tm,)), dma, dma,
         ],
         compiler_params=pltpu.CompilerParams(
-            collective_id=0, has_side_effects=True, vmem_limit_bytes=40 * 2**20
+            collective_id=0, has_side_effects=True, vmem_limit_bytes=56 * 2**20
         ),
         cost_estimate=pl.CostEstimate(
-            flops=2 * 9 * bins * frames * chans * chans, bytes_accessed=5 * 2**20, transcendentals=0
+            flops=2 * 9 * bins * frames * chans * chans, bytes_accessed=15 * 2**20, transcendentals=0
         ),
-    )(
-        lat, mel_noisy, vec(time_shift), vec(first_gain), vec(first_shift),
-        conv_first.reshape(3, 3 * chans, chans), vec(second_gain), vec(second_shift),
-        conv_second.reshape(9, chans, chans), vec(second_bias), vec(out_proj),
-    )
-
-    n_taps, width, mels = pre_full.shape
-    k_taps, outs = up_weight.shape[1], up_weight.shape[2]
-    block = 256
-    vocal = pl.pallas_call(
-        functools.partial(up_kernel, n_tm, frames),
-        grid=(width // block,),
-        out_shape=jax.ShapeDtypeStruct((outs, 4 * frames), BF16),
-        in_specs=[
-            pl.BlockSpec((span, mels), lambda i: (0, 0)),
-            pl.BlockSpec((n_taps, block, mels), lambda i: (0, i, 0)),
-            pl.BlockSpec((1, block), lambda i: (0, i)),
-            pl.BlockSpec((block * k_taps, outs), lambda i: (i, 0)),
-            pl.BlockSpec((1, outs), lambda i: (0, 0)),
-        ],
-        out_specs=pl.BlockSpec((outs, 4 * frames), lambda i: (0, 0)),
-        scratch_shapes=[
-            pltpu.VMEM((span, n_taps * mels), BF16),
-            pltpu.VMEM((block, block * k_taps), BF16),
-            pltpu.VMEM((4 * frames, outs), F32),
-        ],
-        compiler_params=pltpu.CompilerParams(vmem_limit_bytes=40 * 2**20),
-        cost_estimate=pl.CostEstimate(
-            flops=2 * 4 * frames * width * k_taps * outs, bytes_accessed=13 * 2**20, transcendentals=0
-        ),
-    )(mt, pre_full, vec(pre_bias), up_weight.reshape(width * k_taps, outs), vec(up_bias))
-    return (mel_next, vocal)
+    )(*operands)
 
 
 def solution(mesh):

time: 93.2 us -> 47.7 us (0.51)
  waiting for transfers between devices: 20.1 us -> 0 us
  between operations: 14.1 us -> 0.64 us
  local copies, waits for them, and re-layouts: 15.7 us -> 5.53 us
  Pallas kernels: 42.7 us -> 41.2 us
    all_gather x1 -> x0, waiting for transfers between devices: 19.5 us -> none  [shards(): lax.all_gather(jnp.transpose(pre_weight, (1, 0, 2)), 'tm', axis=1, tiled=...]
    unnamed x31 -> x2, local copies, waits for them, and re-layouts: 15.7 us -> 2.99 us
    reshape x2, local copies, waits for them, and re-layouts: 0.01 us -> 2.54 us  [shards(): vec = lambda v: v.reshape(1, -1)]
    pallas_call x2 -> x1, Pallas kernels: 42.7 us -> 41.2 us  [shards(): pl.pallas_call(functools.partial(block_kernel, n_tm, n_f, fused), out_sha...]
  transfers between devices with their start and end apart: 1 -> 0, of which waited for: 1 -> 0; matrix products, arithmetic and copies ran while one was open for 0% -> 0% of each run, Pallas kernels for 36% -> 0%
where the time goes in v2:
time: 47.7 us; the launch traced here: 47.4 us
  Pallas kernels  41.2 us (86%)
  local copies, waits for them, and re-layouts  5.53 us (12%)
  between operations  0.64 us (1%)
    pallas_call x1, Pallas kernels, shards(): pl.pallas_call(functools.partial(block_kernel, n_tm, n_f, fused), out_sha...  41.2 us
    unnamed x2, local copies, waits for them, and re-layouts  2.99 us
    reshape x2, local copies, waits for them, and re-layouts, shards(): vec = lambda v: v.reshape(1, -1)  2.54 us

profile of v2, /device:TPU:0, one launch (start us, length us, event | category | flops | bytes accessed | tf_op | source)
XLA Modules:
  0.0 47.4 jit_solution(10072696395774080104)
XLA Ops:
  0.6 1.2 %reshape.51.up_bias_h = f32[1,384]{1,0:T(1,128)} reshape(f32[384]{0:T(512)} %param.29) | data formatting | bytes 3072 | tf_op jit(solution)/shard_map/reshape | solution.py:521
  1.9 1.3 %reshape.49.pre_bias_h = f32[1,1536]{1,0:T(1,128)} reshape(f32[1536]{0:T(1024)} %param.27) | data formatting | bytes 12288 | tf_op jit(solution)/shard_map/reshape | solution.py:521
  3.2 41.2 %shard_map.158 = (f32[64,64]{1,0:T(8,128)}, bf16[384,256]{1,0:T(8,128)(2,1)}) custom-call(bf16[64,64,256]{2,1,0:T(8,128)(2,1)} %bitcast.13, f32[64,64]{1,0:T(8,128)} %mel_h.1, f32[1,256]{1,0:T(1,128)} %bitcast.17, f32[1,256]{1,0:T(1,128)} %bitcast.18, f32[1,256]{1,0:T(1,128)} %bitcast.19, bf16[3,768,256]{2,1,0:T(8,128)(2,1)} %bitcast.14, f32[1,256]{1,0:T(1,128)} %bitcast.20, ...), custom_call_target="tpu_custom_call" | custom-call | flops 4831838208 | bytes 15728640 | tf_op jit(solution)/shard_map/pallas_call | solution.py:544
  44.4 1.4 %copy.19 = f32[64,64]{1,0:T(8,128)} copy(f32[64,64]{1,0:T(8,128)} %get-tuple-element.4) | data formatting | bytes 32768
  45.8 1.6 %copy.20 = bf16[384,256]{1,0:T(8,128)(2,1)} copy(bf16[384,256]{1,0:T(8,128)(2,1)} %get-tuple-element.5) | data formatting | bytes 393216

commit v3 on v2

--- a/solution.py
+++ b/solution.py
@@ -324,57 +324,62 @@
     put((1 - f) * (bins + 1), silu(halo_b[...].astype(F32), mean, scale, shift), cl, cr)
     spread[f * (bins + 1)] = jnp.zeros(spread.shape[1:], BF16)
 
-    def norm_step(b, c):
-        for u in range(4):
-            at = b * 4 + u
-            x = silu(lat[at].astype(F32), mean, scale, shift)
-            put(at + 1, x, act_l[pl.ds(at, 1), :], act_r[pl.ds(at, 1), :])
-        return c
-
-    lax.fori_loop(0, bins // 4, norm_step, 0)
-
     nb = 8
     moved = tshift[...]
 
-    def conv_step(b, carry):
-        s, q = carry
-        acc = jnp.zeros((nb * frames, chans), F32)
-        for i in range(3):
-            part = spread[pl.ds(b * nb + i, nb)].reshape(nb * frames, 3 * chans)
-            acc = acc + dot(part, w1[i])
-        out = (acc + moved).astype(BF16)
-        first[pl.ds(b * nb, nb)] = out.reshape(nb, frames, chans)
+    def norm_bins(start, end):
+        for at in range(start, min(end, bins)):
+            x = silu(lat[at].astype(F32), mean, scale, shift)
+            put(at + 1, x, act_l[at : at + 1, :], act_r[at : at + 1, :])
+
+    s, q = zero8, zero8
+    norm_bins(0, nb + 1)
+    for b in range(0, bins, nb):
+        part = jnp.concatenate(
+            [spread[b + i : b + i + nb].reshape(nb * frames, 3 * chans) for i in range(3)], axis=1
+        )
+        out = (dot(part, w1[...]) + moved).astype(BF16)
+        norm_bins(b + nb + 1, b + 2 * nb + 1)
+        first[b : b + nb] = out.reshape(nb, frames, chans)
         x = out.astype(F32)
-        return s + fold(x), q + fold(x * x)
-
-    s, q = lax.fori_loop(0, bins // nb, conv_step, (zero8, zero8))
+        s, q = s + fold(x), q + fold(x * x)
     end_stats(stats1, s1_send, s1_recv)
     send_stats(s, q, stats2, s2_send, s2_recv)
 
     if fused:
         gather_forward()
+    vb = 4
+    sub = lax.broadcasted_iota(jnp.int32, (8, frames), 0)
+
+    def direct_step(b, c):
+        raw = lat[pl.ds(b * vb, vb)].reshape(vb * frames, chans)
+        g = dot_nt(direct, raw)
+        for u in range(vb):
+            at = b * vb + u
+            own = mel[pl.ds(at, 1), :] * (1.0 / STEP_SIZE) + const
+            piece = g[8:16, u * frames : (u + 1) * frames]
+            gpad[1, at + 2, :, 0:frames] = jnp.where(sub == 7, own, piece)
+        return c
+
+    lax.fori_loop(0, bins // vb, direct_step, 0)
     mean2, inv2 = take_stats(stats2, s2_send, s2_recv)
     scale2 = inv2 * gain2[...]
     low2 = shift2[...]
-    vb = 4
-    sub = lax.broadcasted_iota(jnp.int32, (8, frames), 0)
 
     def tap_step(b, c):
         x = first[pl.ds(b * vb, vb)].reshape(vb * frames, chans).astype(F32)
         act = silu(x, mean2, scale2, low2).astype(BF16)
-        raw = lat[pl.ds(b * vb, vb)].reshape(vb * frames, chans)
-        g = dot_nt(taps, act) + dot_nt(direct, raw)
+        g = dot_nt(taps, act)
         for u in range(vb):
             at = b * vb + u
-            own = mel[pl.ds(at, 1), :] * (1.0 / STEP_SIZE) + const
             for j in range(3):
                 piece = g[8 * j : 8 * j + 8, u * frames : (u + 1) * frames]
                 if j == 1:
-                    piece = jnp.where(sub == 7, own, piece)
+                    piece = piece + gpad[j, at + 2, :, 0:frames]
                 gpad[j, at + 2, :, 0:frames] = piece
         return c
 
-    lax.fori_loop(0, bins // vb, tap_step, 0)
+    lax.fori_loop(0, bins // vb, tap_step, 0, unroll=4)
     end_stats(stats2, s2_send, s2_recv)
 
     tall = bins + 8
@@ -474,7 +479,9 @@
     for k in range(n_taps):
         made = made + dot_nt(taps_in[:, k * mels : (k + 1) * mels], pre[k].reshape(width, mels))
     pos = lax.broadcasted_iota(jnp.int32, (span, width), 0) - 8 + tm * frames
-    made = made + pre_bias[:, pl.ds(pl.multiple_of(f * width, 128), width)]
+    made = made + jnp.concatenate(
+        [pre_bias[pl.ds(f * (width // 128) + i, 1), :] for i in range(width // 128)], axis=1
+    )
     feats[f] = jnp.where((pos >= 0) & (pos < n_tm * frames), made, 0.0).astype(BF16)
     swap = remote(feats.at[f], feats.at[f], ft_send, ft_recv, partner)
     swap.start()
@@ -503,11 +510,23 @@
     upsample(f)
     swap.wait()
     upsample(other)
-    done = (acc[...] + up_bias[...]).astype(BF16).astype(F32)
+    bias = jnp.concatenate([up_bias[i : i + 1, :] for i in range(up_bias.shape[0])], axis=1)
+    done = acc[...] + bias
     r = lax.broadcasted_iota(jnp.int32, (4 * frames, 4 * frames), 0)
     c = lax.broadcasted_iota(jnp.int32, (4 * frames, 4 * frames), 1)
     perm = (r == lax.rem(c, 4) * frames + c // 4).astype(F32).astype(BF16)
     vocal[...] = dot(jnp.transpose(done).astype(BF16), perm).astype(BF16)
+
+
+def finish_kernel(mel, vocal, mel_out, vocal_out, sems):
+    copies = [
+        pltpu.make_async_copy(mel, mel_out, sems.at[0]),
+        pltpu.make_async_copy(vocal, vocal_out, sems.at[1]),
+    ]
+    for c in copies:
+        c.start()
+    for c in copies:
+        c.wait()
 
 
 def shards(
@@ -536,12 +555,13 @@
         pre = lax.dynamic_slice_in_dim(pre, lax.axis_index("freq") * half, half, axis=1)
     operands = (
         lat, mel_noisy, vec(time_shift), vec(first_gain), vec(first_shift),
-        conv_first.reshape(3, 3 * chans, chans), vec(second_gain), vec(second_shift),
+        conv_first.reshape(9 * chans, chans), vec(second_gain), vec(second_shift),
         conv_second.reshape(9, chans, chans), vec(second_bias), vec(out_proj),
-        pre, vec(pre_bias), up_weight.reshape(-1, outs), vec(up_bias),
+        pre, pre_bias.reshape(-1, 128), up_weight.reshape(-1, outs),
+        up_bias.reshape(-1, 128),
     )
     copies = [pltpu.VMEM(x.shape, x.dtype) for x in operands[:11] + (operands[12], operands[14])]
-    return pl.pallas_call(
+    results = pl.pallas_call(
         functools.partial(block_kernel, n_tm, n_f, fused),
         out_shape=(
             jax.ShapeDtypeStruct((bins, frames), F32),
@@ -588,6 +608,16 @@
             flops=2 * 9 * bins * frames * chans * chans, bytes_accessed=15 * 2**20, transcendentals=0
         ),
     )(*operands)
+    return pl.pallas_call(
+        finish_kernel,
+        out_shape=(
+            jax.ShapeDtypeStruct((bins, frames), F32),
+            jax.ShapeDtypeStruct((outs, 4 * frames), BF16),
+        ),
+        in_specs=[hbm] * 2,
+        out_specs=(hbm, hbm),
+        scratch_shapes=[dma((2,))],
+    )(*results)
 
 
 def solution(mesh):

time: 47.7 us -> 49.6 us (1.040)
  the two profiles are of different devices: /device:TPU:0 before, /device:TPU:21 now
where the time goes in v3:
time: 49.6 us; the launch traced here: 49.5 us
  Pallas kernels  48.7 us (98%)
  between operations  0.8 us (2%)
    pallas_call x1, Pallas kernels, shards(): pl.pallas_call(functools.partial(block_kernel, n_tm, n_f, fused), out_sha...  40.6 us
    pallas_call x1, Pallas kernels, shards(): pl.pallas_call(finish_kernel, out_shape=(jax.ShapeDtypeStruct((bins, fram...  8.07 us

profile of v3, /device:TPU:21, one launch (start us, length us, event | category | flops | bytes accessed | tf_op | source)
XLA Modules:
  0.0 49.5 jit_solution(16268797139921039044)
XLA Ops:
  0.6 40.6 %shard_map.158 = (f32[64,64]{1,0:T(8,128)}, bf16[384,256]{1,0:T(8,128)(2,1)}) custom-call(bf16[64,64,256]{2,1,0:T(8,128)(2,1)} %bitcast.15, f32[64,64]{1,0:T(8,128)} %mel_h.1, f32[1,256]{1,0:T(1,128)} %bitcast.21, f32[1,256]{1,0:T(1,128)} %bitcast.22, f32[1,256]{1,0:T(1,128)} %bitcast.23, bf16[2304,256]{1,0:T(8,128)(2,1)} %bitcast.16, f32[1,256]{1,0:T(1,128)} %bitcast.24, ...), custom_call_target="tpu_custom_call" | custom-call | flops 4831838208 | bytes 15728640 | tf_op jit(solution)/shard_map/pallas_call | solution.py:564
  41.3 8.1 %shard_map.159 = (f32[64,64]{1,0:T(8,128)}, bf16[384,256]{1,0:T(8,128)(2,1)}) custom-call(f32[64,64]{1,0:T(8,128)} %get-tuple-element.4.mel, bf16[384,256]{1,0:T(8,128)(2,1)} %get-tuple-element.5.vocal), custom_call_target="tpu_custom_call" | custom-call | tf_op jit(solution)/shard_map/pallas_call | solution.py:611

commit v4 on v3

--- a/solution.py
+++ b/solution.py
@@ -74,6 +74,12 @@
         return c
 
     lax.fori_loop(1, n, greet, 0)
+    song = lax.axis_index("song")
+    beside = tm + 1 - 2 * lax.rem(tm, 2)
+    across = [{"song": 1 - song, "tm": tm, "freq": f}, {"song": 1 - song, "tm": beside, "freq": f}]
+    if fused:
+        for to in across:
+            pl.semaphore_signal(barrier, inc=1, device_id=to, device_id_type=MESH)
     for c in loads:
         c.start()
     loads[0].wait()
@@ -86,7 +92,7 @@
     stage_l[...] = jnp.sum(jnp.where(sub8 == 0, head, 0.0), axis=1).astype(BF16)
     stage_r[...] = jnp.sum(jnp.where(sub8 == 7, tail, 0.0), axis=1).astype(BF16)
 
-    pl.semaphore_wait(barrier, n - 1)
+    pl.semaphore_wait(barrier, n + 1 if fused else n - 1)
 
     def remote(src, dst, send, recv, to):
         return pltpu.make_async_remote_copy(
@@ -178,16 +184,26 @@
 
     half_n = n_tm // n_f
     slot = lax.rem(tm, half_n)
-    beside = tm + 1 - 2 * lax.rem(tm, 2)
     holder = f == tm // half_n
-
-    def push(k):
+    parity = lax.rem(tm, 2)
+    part_rows = pre.shape[-2] // 2
+
+    def piece_of(d, h):
+        return pre.at[:, d, pl.ds(pl.multiple_of(h * part_rows, 16), part_rows)]
+
+    def push(k, h):
         to = jnp.where(k == 0, beside, lax.rem(tm + 2 * k, n_tm))
-        return remote(pre_h, pre.at[:, slot], p_send.at[k], p_recv.at[slot], {"tm": to, "freq": f})
-
-    def forward(j):
-        d = 2 * j + lax.rem(tm, 2)
-        return d, remote(pre.at[:, d], pre.at[:, d], fw_send.at[j], p_recv.at[d], {"tm": beside, "freq": f})
+        src = pre_h.at[:, pl.ds(pl.multiple_of(h * part_rows, 16), part_rows)]
+        return remote(src, piece_of(slot, h), p_send.at[k, h], p_recv.at[slot, h], {"tm": to, "freq": f})
+
+    def forwards(d):
+        return [
+            remote(piece_of(d, song), piece_of(d, song), fw_send.at[d, i], p_recv.at[d, song], to)
+            for i, to in enumerate([{"tm": beside, "freq": f}] + across)
+        ]
+
+    def arrived(d, h):
+        remote(piece_of(d, h), piece_of(d, h), fw_send.at[d, 0], p_recv.at[d, h], across[0]).wait_recv()
 
     if fused:
         own_pre = pltpu.make_async_copy(pre_h, pre.at[:, slot], own_sem)
@@ -201,19 +217,21 @@
             own_pre.start()
 
             def go(k, c):
-                push(k).start()
+                push(k, song).start()
                 return c
 
             lax.fori_loop(0, n_tm // 2, go, 0)
+            push(0, 1 - song).start()
 
     def gather_forward():
         def go(j, c):
-            d, copy = forward(j)
+            d = 2 * j + parity
 
             @pl.when(d + f * half_n != tm)
             def _():
-                copy.wait_recv()
-                copy.start()
+                arrived(d, song)
+                for copy in forwards(d):
+                    copy.start()
 
             return c
 
@@ -225,20 +243,24 @@
             own_pre.wait()
 
             def wait(k, c):
-                push(k).wait_send()
+                push(k, song).wait_send()
                 return c
 
             lax.fori_loop(0, n_tm // 2, wait, 0)
+            push(0, 1 - song).wait_send()
 
         def rest(j, c):
-            d, copy = forward(j)
+            d = 2 * j + parity
 
             @pl.when(d + f * half_n != tm)
             def _():
-                copy.wait_send()
-
-            e = 2 * j + 1 - lax.rem(tm, 2)
-            remote(pre.at[:, e], pre.at[:, e], fw_send.at[j], p_recv.at[e], {"tm": beside, "freq": f}).wait_recv()
+                arrived(d, 1 - song)
+                for copy in forwards(d):
+                    copy.wait_send()
+
+            e = 2 * j + 1 - parity
+            arrived(e, 0)
+            arrived(e, 1)
             return c
 
         lax.fori_loop(0, half_n // 2, rest, 0)
@@ -249,10 +271,6 @@
     for c in loads[1:]:
         c.wait()
 
-    k_taps = repeat.shape[1] // 128
-    r = lax.broadcasted_iota(jnp.int32, repeat.shape, 0)
-    c = lax.broadcasted_iota(jnp.int32, repeat.shape, 1)
-    repeat[...] = (c // k_taps == r).astype(F32).astype(BF16)
     acc[...] = jnp.zeros(acc.shape, F32)
     gpad[...] = jnp.zeros(gpad.shape, F32)
 
@@ -340,14 +358,14 @@
         )
         out = (dot(part, w1[...]) + moved).astype(BF16)
         norm_bins(b + nb + 1, b + 2 * nb + 1)
+        if fused and b == nb * (bins // nb // 2):
+            gather_forward()
         first[b : b + nb] = out.reshape(nb, frames, chans)
         x = out.astype(F32)
         s, q = s + fold(x), q + fold(x * x)
     end_stats(stats1, s1_send, s1_recv)
     send_stats(s, q, stats2, s2_send, s2_recv)
 
-    if fused:
-        gather_forward()
     vb = 4
     sub = lax.broadcasted_iota(jnp.int32, (8, frames), 0)
 
@@ -362,6 +380,16 @@
         return c
 
     lax.fori_loop(0, bins // vb, direct_step, 0)
+
+    k_taps = repeat.shape[2] // 256
+    r = lax.broadcasted_iota(jnp.int32, repeat.shape[1:], 0)
+    c = lax.broadcasted_iota(jnp.int32, repeat.shape[1:], 1)
+    tap = lax.rem(c, k_taps)
+    chan = lax.rem(c // k_taps, 128)
+    hit = r == jnp.where(tap >= 4, chan + 128, chan)
+    turn = lax.rem(tap, 4) - c // (128 * k_taps)
+    repeat[0] = jnp.where(hit & (turn == 2), 1.0, 0.0).astype(BF16)
+    repeat[1] = jnp.where(hit & (turn == 0), 1.0, 0.0).astype(BF16)
     mean2, inv2 = take_stats(stats2, s2_send, s2_recv)
     scale2 = inv2 * gain2[...]
     low2 = shift2[...]
@@ -489,21 +517,21 @@
 
     group = wide_f.shape[1] // k_taps
     rep = 128 * k_taps
-    lane = lax.broadcasted_iota(jnp.int32, (span, rep), 1)
-    upper = lax.rem(lane, k_taps) < 4
-    phase = lax.rem(lane[0:frames], 4)
 
     def upsample(h):
+        x = feats[h].astype(F32)
+        mid = x[8 : 8 + frames].astype(BF16)
+        prev = pltpu.roll(x, 1, 0)[8 : 8 + frames].astype(BF16)
+        later = pltpu.roll(x, span - 1, 0)[8 : 8 + frames].astype(BF16)
         for g in range(width // group):
             for t in range(group // 128):
-                at = g * group + t * 128
-                wide = dot(feats[h, :, at : at + 128], repeat[...])
-                wide = jnp.where(upper, wide, pltpu.roll(wide, 1, 0))
-                for p in range(4):
-                    start = 8 + (1 if p >= 2 else 0)
-                    wide_f[p * frames : (p + 1) * frames, t * rep : (t + 1) * rep] = jnp.where(
-                        phase == (p + 2) % 4, wide[start : start + frames], 0.0
-                    ).astype(BF16)
+                cols = slice(g * group + t * 128, g * group + t * 128 + 128)
+                for half_of, pair in enumerate(((mid, prev), (later, mid))):
+                    both = jnp.concatenate([v[:, cols] for v in pair], axis=1)
+                    wide = dot(both, repeat[half_of]).astype(BF16)
+                    for p in range(2):
+                        top = (2 * half_of + p) * frames
+                        wide_f[top : top + frames, t * rep : (t + 1) * rep] = wide[:, p * rep : (p + 1) * rep]
             row = pl.multiple_of((h * width + g * group) * k_taps, 128)
             acc[...] += dot(wide_f[...], up[pl.ds(row, group * k_taps), :])
 
@@ -516,17 +544,6 @@
     c = lax.broadcasted_iota(jnp.int32, (4 * frames, 4 * frames), 1)
     perm = (r == lax.rem(c, 4) * frames + c // 4).astype(F32).astype(BF16)
     vocal[...] = dot(jnp.transpose(done).astype(BF16), perm).astype(BF16)
-
-
-def finish_kernel(mel, vocal, mel_out, vocal_out, sems):
-    copies = [
-        pltpu.make_async_copy(mel, mel_out, sems.at[0]),
-        pltpu.make_async_copy(vocal, vocal_out, sems.at[1]),
-    ]
-    for c in copies:
-        c.start()
-    for c in copies:
-        c.wait()
 
 
 def shards(
@@ -546,7 +563,7 @@
     n_taps, rows, mels = pre.shape
     k_taps, outs = up_weight.shape[1], up_weight.shape[2]
     half = n_tm * rows // n_f
-    fused = rows % 16 == 0 and n_tm % 4 == 0
+    fused = rows % 32 == 0 and n_tm % 4 == 0 and lax.axis_size("song") == 2
     if fused:
         held = (n_taps, n_tm // n_f, rows, mels)
     else:
@@ -561,7 +578,7 @@
         up_bias.reshape(-1, 128),
     )
     copies = [pltpu.VMEM(x.shape, x.dtype) for x in operands[:11] + (operands[12], operands[14])]
-    results = pl.pallas_call(
+    return pl.pallas_call(
         functools.partial(block_kernel, n_tm, n_f, fused),
         out_shape=(
             jax.ShapeDtypeStruct((bins, frames), F32),
@@ -592,14 +609,14 @@
             pltpu.VMEM((2, 8, 128), F32),
             pltpu.VMEM((128, 128), F32),
             pltpu.VMEM((span, n_taps * mels), BF16),
-            pltpu.VMEM((128, 128 * k_taps), BF16),
+            pltpu.VMEM((2, 256, 256 * k_taps), BF16),
             pltpu.VMEM((2, span, half), BF16),
             pltpu.VMEM((4 * frames, 384 * k_taps), BF16),
             pltpu.VMEM((4 * frames, outs), F32),
             dma((13,)), dma, dma,
             dma((n,)), dma((n,)), dma((n,)), dma((n,)),
             dma((5,)), dma((5,)), dma((5,)), dma((5,)),
-            dma((n_tm,)), dma((n_tm,)), dma((n_tm,)), dma, dma,
+            dma((n_tm // 2, 2)), dma((n_tm // 2, 2)), dma((n_tm // 2, 3)), dma, dma,
         ],
         compiler_params=pltpu.CompilerParams(
             collective_id=0, has_side_effects=True, vmem_limit_bytes=56 * 2**20
@@ -608,16 +625,6 @@
             flops=2 * 9 * bins * frames * chans * chans, bytes_accessed=15 * 2**20, transcendentals=0
         ),
     )(*operands)
-    return pl.pallas_call(
-        finish_kernel,
-        out_shape=(
-            jax.ShapeDtypeStruct((bins, frames), F32),
-            jax.ShapeDtypeStruct((outs, 4 * frames), BF16),
-        ),
-        in_specs=[hbm] * 2,
-        out_specs=(hbm, hbm),
-        scratch_shapes=[dma((2,))],
-    )(*results)
 
 
 def solution(mesh):

time: 49.6 us -> 47.5 us (0.958)
  the two profiles are of different devices: /device:TPU:21 before, /device:TPU:0 now
where the time goes in v4:
time: 47.5 us; the launch traced here: 46.7 us
  Pallas kernels  43 us (91%)
  local copies, waits for them, and re-layouts  2.99 us (6%)
  between operations  0.65 us (1%)
    pallas_call x1, Pallas kernels, shards(): pl.pallas_call(functools.partial(block_kernel, n_tm, n_f, fused), out_sha...  43 us
    unnamed x2, local copies, waits for them, and re-layouts  2.99 us

profile of v4, /device:TPU:0, one launch (start us, length us, event | category | flops | bytes accessed | tf_op | source)
XLA Modules:
  0.0 46.7 jit_solution(13016292304355563698)
XLA Ops:
  0.6 43.0 %shard_map.158 = (f32[64,64]{1,0:T(8,128)}, bf16[384,256]{1,0:T(8,128)(2,1)}) custom-call(bf16[64,64,256]{2,1,0:T(8,128)(2,1)} %bitcast.15, f32[64,64]{1,0:T(8,128)} %mel_h.1, f32[1,256]{1,0:T(1,128)} %bitcast.21, f32[1,256]{1,0:T(1,128)} %bitcast.22, f32[1,256]{1,0:T(1,128)} %bitcast.23, bf16[2304,256]{1,0:T(8,128)(2,1)} %bitcast.16, f32[1,256]{1,0:T(1,128)} %bitcast.24, ...), custom_call_target="tpu_custom_call" | custom-call | flops 4831838208 | bytes 15728640 | tf_op jit(solution)/shard_map/pallas_call | solution.py:581
  43.7 1.4 %copy.19 = f32[64,64]{1,0:T(8,128)} copy(f32[64,64]{1,0:T(8,128)} %get-tuple-element.4) | data formatting | bytes 32768
  45.1 1.6 %copy.20 = bf16[384,256]{1,0:T(8,128)(2,1)} copy(bf16[384,256]{1,0:T(8,128)(2,1)} %get-tuple-element.5) | data formatting | bytes 393216

commit v5 on v4

--- a/solution.py
+++ b/solution.py
@@ -82,6 +82,19 @@
             pl.semaphore_signal(barrier, inc=1, device_id=to, device_id_type=MESH)
     for c in loads:
         c.start()
+    acc[...] = jnp.zeros(acc.shape, F32)
+    gpad[...] = jnp.zeros(gpad.shape, F32)
+
+    k_taps = repeat.shape[2] // 256
+    r = lax.broadcasted_iota(jnp.int32, repeat.shape[1:], 0)
+    c = lax.broadcasted_iota(jnp.int32, (1, repeat.shape[2]), 1)
+    tap = lax.rem(c, k_taps)
+    chan = lax.rem(c // k_taps, 128)
+    source = jnp.where(tap >= 4, chan + 128, chan)
+    turn = lax.rem(tap, 4) - c // (128 * k_taps)
+    for g in range(2):
+        wanted = jnp.where(turn == 2 - 2 * g, source, -1)
+        repeat[g] = jnp.where(r == wanted, 1.0, 0.0).astype(BF16)
     loads[0].wait()
     load_up = pltpu.make_async_copy(up_h, up, up_sem)
     load_up.start()
@@ -271,8 +284,6 @@
     for c in loads[1:]:
         c.wait()
 
-    acc[...] = jnp.zeros(acc.shape, F32)
-    gpad[...] = jnp.zeros(gpad.shape, F32)
 
     p_row = proj[...]
     hi, mid, low = [x.astype(F32) for x in three_parts(p_row)]
@@ -358,14 +369,14 @@
         )
         out = (dot(part, w1[...]) + moved).astype(BF16)
         norm_bins(b + nb + 1, b + 2 * nb + 1)
-        if fused and b == nb * (bins // nb // 2):
-            gather_forward()
         first[b : b + nb] = out.reshape(nb, frames, chans)
         x = out.astype(F32)
         s, q = s + fold(x), q + fold(x * x)
     end_stats(stats1, s1_send, s1_recv)
     send_stats(s, q, stats2, s2_send, s2_recv)
 
+    if fused:
+        gather_forward()
     vb = 4
     sub = lax.broadcasted_iota(jnp.int32, (8, frames), 0)
 
@@ -381,15 +392,6 @@
 
     lax.fori_loop(0, bins // vb, direct_step, 0)
 
-    k_taps = repeat.shape[2] // 256
-    r = lax.broadcasted_iota(jnp.int32, repeat.shape[1:], 0)
-    c = lax.broadcasted_iota(jnp.int32, repeat.shape[1:], 1)
-    tap = lax.rem(c, k_taps)
-    chan = lax.rem(c // k_taps, 128)
-    hit = r == jnp.where(tap >= 4, chan + 128, chan)
-    turn = lax.rem(tap, 4) - c // (128 * k_taps)
-    repeat[0] = jnp.where(hit & (turn == 2), 1.0, 0.0).astype(BF16)
-    repeat[1] = jnp.where(hit & (turn == 0), 1.0, 0.0).astype(BF16)
     mean2, inv2 = take_stats(stats2, s2_send, s2_recv)
     scale2 = inv2 * gain2[...]
     low2 = shift2[...]

time: 47.5 us -> 44.6 us (0.939)
  the two profiles are of different devices: /device:TPU:0 before, /device:TPU:1 now
where the time goes in v5:
time: 44.6 us; the launch traced here: 44.4 us
  Pallas kernels  40.8 us (91%)
  local copies, waits for them, and re-layouts  2.99 us (7%)
  between operations  0.65 us (1%)
    pallas_call x1, Pallas kernels, shards(): pl.pallas_call(functools.partial(block_kernel, n_tm, n_f, fused), out_sha...  40.8 us
    unnamed x2, local copies, waits for them, and re-layouts  2.99 us

profile of v5, /device:TPU:1, one launch (start us, length us, event | category | flops | bytes accessed | tf_op | source)
XLA Modules:
  0.0 44.4 jit_solution(10006155136753361684)
XLA Ops:
  0.6 40.8 %shard_map.158 = (f32[64,64]{1,0:T(8,128)}, bf16[384,256]{1,0:T(8,128)(2,1)}) custom-call(bf16[64,64,256]{2,1,0:T(8,128)(2,1)} %bitcast.15, f32[64,64]{1,0:T(8,128)} %mel_h.1, f32[1,256]{1,0:T(1,128)} %bitcast.21, f32[1,256]{1,0:T(1,128)} %bitcast.22, f32[1,256]{1,0:T(1,128)} %bitcast.23, bf16[2304,256]{1,0:T(8,128)(2,1)} %bitcast.16, f32[1,256]{1,0:T(1,128)} %bitcast.24, ...), custom_call_target="tpu_custom_call" | custom-call | flops 4831838208 | bytes 15728640 | tf_op jit(solution)/shard_map/pallas_call | solution.py:583
  41.4 1.4 %copy.19 = f32[64,64]{1,0:T(8,128)} copy(f32[64,64]{1,0:T(8,128)} %get-tuple-element.4) | data formatting | bytes 32768
  42.8 1.6 %copy.20 = bf16[384,256]{1,0:T(8,128)(2,1)} copy(bf16[384,256]{1,0:T(8,128)(2,1)} %get-tuple-element.5) | data formatting | bytes 393216

commit v6 on v5

--- a/solution.py
+++ b/solution.py
@@ -73,7 +73,7 @@
         pl.semaphore_signal(barrier, inc=1, device_id=peer_of(k)[1], device_id_type=MESH)
         return c
 
-    lax.fori_loop(1, n, greet, 0)
+    lax.fori_loop(1, n, greet, 0, unroll=n <= 16)
     song = lax.axis_index("song")
     beside = tm + 1 - 2 * lax.rem(tm, 2)
     across = [{"song": 1 - song, "tm": tm, "freq": f}, {"song": 1 - song, "tm": beside, "freq": f}]
@@ -105,8 +105,6 @@
     stage_l[...] = jnp.sum(jnp.where(sub8 == 0, head, 0.0), axis=1).astype(BF16)
     stage_r[...] = jnp.sum(jnp.where(sub8 == 7, tail, 0.0), axis=1).astype(BF16)
 
-    pl.semaphore_wait(barrier, n + 1 if fused else n - 1)
-
     def remote(src, dst, send, recv, to):
         return pltpu.make_async_remote_copy(
             src_ref=src, dst_ref=dst, send_sem=send, recv_sem=recv, device_id=to, device_id_type=MESH
@@ -117,7 +115,6 @@
     to_right = [{"tm": tm + 1, "freq": f}, {"tm": tm + 1, "freq": other}]
     partner = {"tm": tm, "freq": other}
     h_bin = remote(lat.at[(1 - f) * (bins - 1)], halo_b, h_send.at[0], h_recv.at[0], partner)
-    h_bin.start()
     go_left = [
         remote(stage_l, halo_r, h_send.at[1], h_recv.at[1], to_left[0]),
         remote(stage_l.at[pl.ds(edge, 16)], corner_r, h_send.at[2], h_recv.at[2], to_left[1]),
@@ -127,16 +124,6 @@
         remote(stage_r.at[pl.ds(edge, 16)], corner_l, h_send.at[4], h_recv.at[4], to_right[1]),
     ]
 
-    @pl.when(has_left)
-    def _():
-        for c in go_left:
-            c.start()
-
-    @pl.when(has_right)
-    def _():
-        for c in go_right:
-            c.start()
-
     def fold(x):
         return jnp.sum(x.reshape(-1, 8, chans), axis=0)
 
@@ -158,7 +145,7 @@
             remote(stats.at[me], stats.at[me], send.at[k], recv.at[me], to).start()
             return c
 
-        lax.fori_loop(1, n, go, 0)
+        lax.fori_loop(1, n, go, 0, unroll=n <= 16)
 
     def take_stats(stats, send, recv):
         def wait(k, c):
@@ -166,7 +153,7 @@
             remote(stats.at[me], stats.at[p], send.at[k], recv.at[p], to).wait_recv()
             return c
 
-        lax.fori_loop(1, n, wait, 0)
+        lax.fori_loop(1, n, wait, 0, unroll=n <= 16)
         total = jnp.sum(stats[...], axis=0)
         both = jnp.concatenate(
             [
@@ -191,9 +178,21 @@
             remote(stats.at[me], stats.at[me], send.at[k], recv.at[me], to).wait_send()
             return c
 
-        lax.fori_loop(1, n, wait, 0)
-
+        lax.fori_loop(1, n, wait, 0, unroll=n <= 16)
+
+    pl.semaphore_wait(barrier, n + 1 if fused else n - 1)
     send_stats(s, q, stats1, s1_send, s1_recv)
+    h_bin.start()
+
+    @pl.when(has_left)
+    def _():
+        for c in go_left:
+            c.start()
+
+    @pl.when(has_right)
+    def _():
+        for c in go_right:
+            c.start()
 
     half_n = n_tm // n_f
     slot = lax.rem(tm, half_n)
@@ -372,8 +371,8 @@
         first[b : b + nb] = out.reshape(nb, frames, chans)
         x = out.astype(F32)
         s, q = s + fold(x), q + fold(x * x)
+    send_stats(s, q, stats2, s2_send, s2_recv)
     end_stats(stats1, s1_send, s1_recv)
-    send_stats(s, q, stats2, s2_send, s2_recv)
 
     if fused:
         gather_forward()

time: 44.6 us -> 44.1 us (0.989)
  Pallas kernels: 40.8 us -> 40.3 us
    pallas_call x1, Pallas kernels: 40.8 us -> 40.3 us  [shards(): pl.pallas_call(functools.partial(block_kernel, n_tm, n_f, fused), out_sha...]
where the time goes in v6:
time: 44.1 us; the launch traced here: 43.9 us
  Pallas kernels  40.3 us (91%)
  local copies, waits for them, and re-layouts  2.99 us (7%)
  between operations  0.65 us (1%)
    pallas_call x1, Pallas kernels, shards(): pl.pallas_call(functools.partial(block_kernel, n_tm, n_f, fused), out_sha...  40.3 us
    unnamed x2, local copies, waits for them, and re-layouts  2.99 us

profile of v6, /device:TPU:1, one launch (start us, length us, event | category | flops | bytes accessed | tf_op | source)
XLA Modules:
  0.0 43.9 jit_solution(9939821782917094791)
XLA Ops:
  0.6 40.3 %shard_map.158 = (f32[64,64]{1,0:T(8,128)}, bf16[384,256]{1,0:T(8,128)(2,1)}) custom-call(bf16[64,64,256]{2,1,0:T(8,128)(2,1)} %bitcast.15, f32[64,64]{1,0:T(8,128)} %mel_h.1, f32[1,256]{1,0:T(1,128)} %bitcast.21, f32[1,256]{1,0:T(1,128)} %bitcast.22, f32[1,256]{1,0:T(1,128)} %bitcast.23, bf16[2304,256]{1,0:T(8,128)(2,1)} %bitcast.16, f32[1,256]{1,0:T(1,128)} %bitcast.24, ...), custom_call_target="tpu_custom_call" | custom-call | flops 4831838208 | bytes 15728640 | tf_op jit(solution)/shard_map/pallas_call | solution.py:582
  40.9 1.4 %copy.19 = f32[64,64]{1,0:T(8,128)} copy(f32[64,64]{1,0:T(8,128)} %get-tuple-element.4) | data formatting | bytes 32768
  42.3 1.6 %copy.20 = bf16[384,256]{1,0:T(8,128)(2,1)} copy(bf16[384,256]{1,0:T(8,128)(2,1)} %get-tuple-element.5) | data formatting | bytes 393216
